TPU v7x, 128 devices: a whole 4x4x4 slice. The times are simulated.
128 devices in a mesh: tm: 8 (over y_lo, z), row: 16 (over x, y_hi, core).
Axes of the slice: x: 4, y: 4 (y_hi: 2, y_lo: 2; y = y_hi * 2 + y_lo), z: 4, core: 2. Of those that a mesh axis runs over, the one named last changes fastest.
Arguments:
- features: bfloat16 [32, 64, 64, 512], P('tm', 'row'), may hold values from -200 to 200
- norm_gain: float32 [512], replicated, may hold values from 0.1 to 1.9
- norm_bias: float32 [512], replicated, may hold values from -3 to 3
- latent_kernel: bfloat16 [16, 3, 3, 3, 512], replicated, may hold values from -0.0546875 to 0.0546875
- latent_bias: float32 [16], replicated, may hold values from -3 to 3
- token_mask: int32 [32, 64, 64], P('tm', 'row'), may hold values 0 or 1
- embed_weight: bfloat16 [16, 2048], replicated, may hold values from -1.5 to 1.5
- mask_token: float32 [2048], replicated, may hold values from -5 to 5
- pos_embed: bfloat16 [32, 64, 64, 2048], P('tm', 'row'), may hold values from -3 to 3
- query_weight: bfloat16 [2048, 1024], replicated, may hold values from -0.125 to 0.125
- key_weight: bfloat16 [2048, 1024], replicated, may hold values from -0.125 to 0.125
- value_weight: bfloat16 [2048, 1024], replicated, may hold values from -0.125 to 0.125
- logit_scale: float32 [8], replicated, may hold values from 8 to 32
- pattern: int32 [32, 32, 4], P('tm', 'row'), may hold values from -1 to 1023, as said below
Outputs:
- attended: bfloat16 [32, 64, 64, 1024], P('tm', 'row')
Inputs may be any that keep to these rules, and one draw needn't show every extreme that they name: `pattern`: row (t, p) lists key blocks for the query block of frame t and row pair p (block id t * 32 + p): first that block itself, then distinct blocks whose frame differs from t by at most one and whose row pair differs from p by at most one; the rest of the row is -1. On every device the first row pair of its first frame lists 4 blocks.
All inputs are finite; a program needn't handle non-finite values. No bound on the sum of `token_mask` on one device may be relied on, other than what follows from the above.
Results may differ from a plain program's by a relative error of at most 0.0085.
Values may be sent and summed in bfloat16 or wider, within the bound.
A program may use at most 128 MiB of HBM per device.

v0:
```python
import jax
import jax.numpy as jnp
from jax import lax
from jax.sharding import Mesh
from jax.sharding import PartitionSpec as P

GROUPS = 32
TM = ("tm_0", "tm_1")
ROW = ("row_0", "row_1", "row_2")
TM_ROW = ("tm_0", "tm_1", "row_0", "row_1", "row_2")


def by_axis(shard, axes):
    for axis in axes:
        shard = lax.psum(shard, axis)
    return shard


def with_halo(cells, sides, width):
    for axis, dim in sides:
        count = lax.axis_size(axis)
        ends = count - 1
        head = lax.slice_in_dim(cells, 0, width, axis=dim)
        tail = lax.slice_in_dim(cells, cells.shape[dim] - width, cells.shape[dim], axis=dim)
        cells = jnp.concatenate(
            [
                lax.ppermute(tail, axis, [(i, (i + 1) % count) for i in range(ends)]),
                cells,
                lax.ppermute(head, axis, [((i + 1) % count, i) for i in range(ends)]),
            ],
            axis=dim,
        )
    return cells


def unit_heads(values, head_count):
    shaped = values.astype(jnp.float32).reshape(values.shape[0], head_count, -1)
    normal = shaped * lax.rsqrt(jnp.mean(shaped * shaped, axis=-1, keepdims=True) + 1e-06)
    return normal.astype(jnp.bfloat16).reshape(values.shape[0], -1)


def per_device(
    features,
    norm_gain,
    norm_bias,
    latent_kernel,
    latent_bias,
    token_mask,
    embed_weight,
    mask_token,
    pos_embed,
    query_weight,
    key_weight,
    value_weight,
    logit_scale,
    pattern,
):
    frames, slab_rows, row_width, channels = features.shape
    per_group = channels // GROUPS
    time_count = lax.axis_size(TM)
    row_count = lax.axis_size(ROW)
    time_index = lax.axis_index(TM)
    row_index = lax.axis_index(ROW)
    widened = features.astype(jnp.float32)
    grouped = widened.reshape(-1, GROUPS, per_group)
    totals, squares = (
        by_axis(jnp.sum(grouped, axis=(0, 2)), TM_ROW),
        by_axis(jnp.sum(grouped * grouped, axis=(0, 2)), TM_ROW),
    )
    cell_count = frames * time_count * slab_rows * row_count * row_width * per_group
    average = totals / cell_count
    variance = squares / cell_count - average * average
    inverse = lax.rsqrt(variance + 1e-06)
    channel_scale = jnp.repeat(inverse, per_group) * norm_gain
    channel_shift = norm_bias - jnp.repeat(average * inverse, per_group) * norm_gain
    border = with_halo(features, ((TM, 0), (ROW, 1)), 1)
    frame_ids = time_index * frames + jnp.arange(frames + 2) - 1
    row_ids = row_index * slab_rows + jnp.arange(slab_rows + 2) - 1
    frame_inside = (frame_ids >= 0) & (frame_ids < frames * time_count)
    row_inside = (row_ids >= 0) & (row_ids < slab_rows * row_count)
    inside = frame_inside[:, None] & row_inside[None, :]
    normed = jax.nn.silu(border.astype(jnp.float32) * channel_scale + channel_shift)
    extended = jnp.where(inside[:, :, None, None], normed, 0.0).astype(jnp.bfloat16)
    latent_count = latent_kernel.shape[0]
    padded = jnp.pad(extended, ((0, 0), (0, 0), (1, 1), (0, 0)))
    kernel = latent_kernel.transpose(4, 1, 2, 3, 0).reshape(channels, 27 * latent_count)
    products = jnp.dot(padded.reshape(-1, channels), kernel, preferred_element_type=jnp.float32)
    products = products.reshape(frames + 2, slab_rows + 2, row_width + 2, 3, 3, 3, latent_count)
    summed = jnp.zeros((frames, slab_rows, row_width, latent_count), jnp.float32)
    for offset_t in range(3):
        for offset_h in range(3):
            for offset_w in range(3):
                summed = (
                    summed
                    + products[
                        offset_t : offset_t + frames,
                        offset_h : offset_h + slab_rows,
                        offset_w : offset_w + row_width,
                        offset_t,
                        offset_h,
                        offset_w,
                    ]
                )
    latent = (summed + latent_bias).astype(jnp.bfloat16)
    tokens = jnp.dot(
        latent.reshape(-1, latent_count), embed_weight, preferred_element_type=jnp.float32
    )
    tokens = jnp.where(token_mask.reshape(-1, 1) == 1, mask_token, tokens)
    tokens = tokens + pos_embed.reshape(-1, pos_embed.shape[-1]).astype(jnp.float32)
    centred = tokens - jnp.mean(tokens, axis=-1, keepdims=True)
    hidden = (
        centred * lax.rsqrt(jnp.mean(centred * centred, axis=-1, keepdims=True) + 1e-05)
    ).astype(jnp.bfloat16)
    head_count = logit_scale.shape[0]
    inner = query_weight.shape[1]
    head_size = inner // head_count
    unit_query = unit_heads(
        jnp.dot(hidden, query_weight, preferred_element_type=jnp.float32).astype(jnp.bfloat16),
        head_count,
    )
    unit_key = unit_heads(
        jnp.dot(hidden, key_weight, preferred_element_type=jnp.float32).astype(jnp.bfloat16),
        head_count,
    )
    value_raw = jnp.dot(hidden, value_weight, preferred_element_type=jnp.float32).astype(
        jnp.bfloat16
    )
    row_pairs = slab_rows // 2
    block_span = 2 * row_width
    block_count = frames * row_pairs
    query_blocks = unit_query.reshape(block_count, block_span, head_count, head_size)
    stacked = jnp.stack(
        [
            unit_key.reshape(frames, row_pairs, block_span, inner),
            value_raw.reshape(frames, row_pairs, block_span, inner),
        ],
        axis=2,
    )
    nearby = with_halo(stacked, ((TM, 0), (ROW, 1)), 1)
    nearby = nearby.reshape((frames + 2) * (row_pairs + 2), 2, block_span, head_count, head_size)
    pair_total = row_pairs * row_count
    listed = pattern.reshape(block_count, -1)
    usable = listed >= 0
    clamped = jnp.maximum(listed, 0)
    key_frame = clamped // pair_total - time_index * frames + 1
    key_pair = clamped % pair_total - row_index * row_pairs + 1
    own_frame = jnp.arange(block_count) // row_pairs + 1
    own_pair = jnp.arange(block_count) % row_pairs + 1
    own_local = (own_frame * (row_pairs + 2) + own_pair)[:, None]
    where_local = jnp.where(usable, key_frame * (row_pairs + 2) + key_pair, own_local)
    scale = logit_scale / head_size

    def attend_slot(slot_index, state_pair):
        numerator, denominator = state_pair
        chosen = jnp.take(
            nearby, lax.dynamic_index_in_dim(where_local, slot_index, 1, keepdims=False), axis=0
        )
        live_slot = lax.dynamic_index_in_dim(usable, slot_index, 1, keepdims=False).astype(
            jnp.float32
        )
        scores = (
            jnp.einsum(
                "bqhd,bkhd->bhqk", query_blocks, chosen[:, 0], preferred_element_type=jnp.float32
            )
            * scale[None, :, None, None]
        )
        weights = jnp.exp(scores) * live_slot[:, None, None, None]
        denominator = denominator + jnp.sum(weights, axis=-1)
        numerator = numerator + jnp.einsum(
            "bhqk,bkhd->bqhd",
            weights.astype(jnp.bfloat16),
            chosen[:, 1],
            preferred_element_type=jnp.float32,
        )
        return (numerator, denominator)

    loop_limit = listed.shape[1]
    start_numerator = jnp.zeros((block_count, block_span, head_count, head_size), jnp.float32)
    start_denominator = jnp.zeros((block_count, head_count, block_span), jnp.float32)
    numerator, denominator = lax.fori_loop(
        0, loop_limit, attend_slot, (start_numerator, start_denominator)
    )
    attended = numerator / jnp.transpose(denominator, (0, 2, 1))[..., None]
    return attended.astype(jnp.bfloat16).reshape(frames, slab_rows, row_width, inner)


def solution(mesh):
    split = Mesh(mesh.devices.reshape(2, 4, 4, 2, 2), ("tm_0", "tm_1", "row_0", "row_1", "row_2"))
    return jax.shard_map(
        per_device,
        mesh=split,
        in_specs=(
            P(TM, ROW, None, None),
            P(),
            P(),
            P(),
            P(),
            P(TM, ROW, None),
            P(),
            P(),
            P(TM, ROW, None, None),
            P(),
            P(),
            P(),
            P(),
            P(TM, ROW, None),
        ),
        out_specs=P(TM, ROW, None, None),
        check_vma=False,
    )
```

profile of v0, /device:TPU:11, one launch (start us, length us, event | category | flops | bytes accessed | tf_op | source)
XLA Modules:
  0.0 310.0 jit_solution(7728738471096017777)
XLA Ops:
  1.1 5.6 %collective-permute-start.1 = (bf16[1,4,64,512]{3,2,1,0:T(8,128)(2,1)S(1)}, bf16[1,4,64,512]{3,2,1,0:T(8,128)(2,1)S(1)}, u32[]{:S(2)}, u32[]{:S(2)}) collective-permute-start(bf16[1,4,64,512]{3,2,1,0:T(8,128)(2,1)S(1)} %get-tuple-element.224), channel_id=1, source_target_pairs={{16,0},{32,16},{48,32},{64,48},{80,64},{96,80},{112,96},{17,1},{33... | collective-permute-start | bytes 786440 | tf_op jit(solution)/shard_map/ppermute | solution.py:29
  6.7 1.9 collective-permute-start
  8.6 1.6 convert_reduce_fusion
  11.3 4.1 %all-reduce.5 = (f32[32]{0:T(128)S(1)}, f32[32]{0:T(128)S(1)}) all-reduce(f32[32]{0:T(128)S(1)} %reduce_sum.83, f32[32]{0:T(128)S(1)} %reduce_sum.86), channel_id=1, replica_groups=mesh['tm_0'=2,'tm_1'=4,'row_0'=4,'row_1'=2,'row_2'=2] {'tm_0'}, use_global_device_ids=true, to_apply=%region_2.0 | all-reduce | flops 64 | bytes 512 | tf_op jit(solution)/shard_map/psum | solution.py:15
  15.4 8.2 %all-reduce.2 = (f32[32]{0:T(128)S(1)}, f32[32]{0:T(128)S(1)}) all-reduce(f32[32]{0:T(128)S(1)} %get-tuple-element.200, f32[32]{0:T(128)S(1)} %get-tuple-element.201), channel_id=1, replica_groups=mesh['tm_0'=2,'tm_1'=4,'row_0'=4,'row_1'=2,'row_2'=2] {'tm_1'}, use_global_device_ids=true, to_apply=%region_3.0 | all-reduce | flops 64 | bytes 512 | tf_op jit(solution)/shard_map/psum | solution.py:15
  23.6 6.6 %all-reduce.1 = (f32[32]{0:T(128)S(1)}, f32[32]{0:T(128)S(1)}) all-reduce(f32[32]{0:T(128)S(1)} %get-tuple-element.194, f32[32]{0:T(128)S(1)} %get-tuple-element.195), channel_id=1, replica_groups=mesh['tm_0'=2,'tm_1'=4,'row_0'=4,'row_1'=2,'row_2'=2] {'row_0'}, use_global_device_ids=true, to_apply=%region_4.0 | all-reduce | flops 64 | bytes 512 | tf_op jit(solution)/shard_map/psum | solution.py:15
  30.2 5.3 %all-reduce.4 = (f32[32]{0:T(128)S(1)}, f32[32]{0:T(128)S(1)}) all-reduce(f32[32]{0:T(128)S(1)} %get-tuple-element.192, f32[32]{0:T(128)S(1)} %get-tuple-element.193), channel_id=1, replica_groups=mesh['tm_0'=2,'tm_1'=4,'row_0'=4,'row_1'=2,'row_2'=2] {'row_1'}, use_global_device_ids=true, to_apply=%region_5.0 | all-reduce | flops 64 | bytes 512 | tf_op jit(solution)/shard_map/psum | solution.py:15
  35.5 9.4 %all-reduce.3 = (f32[32]{0:T(128)S(1)}, f32[32]{0:T(128)S(1)}) all-reduce(f32[32]{0:T(128)S(1)} %get-tuple-element.198, f32[32]{0:T(128)S(1)} %get-tuple-element.199), channel_id=1, replica_groups=mesh['tm_0'=2,'tm_1'=4,'row_0'=4,'row_1'=2,'row_2'=2] {'row_2'}, use_global_device_ids=true, to_apply=%region_6.0 | all-reduce | flops 64 | bytes 512 | tf_op jit(solution)/shard_map/psum | solution.py:15
  46.8 4.5 %collective-permute-start.2 = (bf16[6,1,64,512]{3,2,1,0:T(8,128)(2,1)S(1)}, bf16[6,1,64,512]{3,2,1,0:T(8,128)(2,1)S(1)}, u32[]{:S(2)}, u32[]{:S(2)}) collective-permute-start(bf16[6,1,64,512]{3,2,1,0:T(8,128)(2,1)S(1)} %get-tuple-element.222), channel_id=1, source_target_pairs={{0,1},{1,2},{2,3},{3,4},{4,5},{5,6},{6,7},{7,8},{8,9},{9,10},{10,1... | collective-permute-start | bytes 1179656 | tf_op jit(solution)/shard_map/ppermute | solution.py:27
  51.2 1.9 collective-permute-start.3
  53.2 2.7 collective-permute-done.2
  55.9 6.3 %collective-permute-done.3 = bf16[6,1,64,512]{3,2,1,0:T(8,128)(2,1)S(1)} collective-permute-done((bf16[6,1,64,512]{3,2,1,0:T(8,128)(2,1)S(1)}, bf16[6,1,64,512]{3,2,1,0:T(8,128)(2,1)S(1)}, u32[]{:S(2)}, u32[]{:S(2)}) %collective-permute-start.3) | collective-permute-done | bytes 393248 | tf_op jit(solution)/shard_map/ppermute | solution.py:29
  62.2 1.6 select_convert_fusion
  63.8 2.3 fusion.4
  69.2 3.8 %fusion.27 = (f32[1024]{0:T(1024)S(1)}, f32[1024,2048]{1,0:T(8,128)S(1)}) fusion(bf16[1024,2048]{1,0:T(8,128)(2,1)} %bitcast.122, bf16[16,2048]{1,0:T(8,128)(2,1)S(1)} %copy-done.13, f32[1024,16]{0,1:T(8,128)S(1)} %squeeze.114, f32[1024,16]{0,1:T(8,128)S(1)} %squeeze.113, f32[1024,16]{0,1:T(8,128)S(1)} %squeeze.112, f32[1024,16]{0,1:T(8,128)S(1)} %squeeze.111, ...), kind=kOutput, calls=%fused_computation.103 | convolution fusion | flops 75693056 | bytes 13382720 | tf_op jit(solution)/shard_map/dot_general | solution.py:105
  76.2 5.7 %convolution_convert_fusion.1 = bf16[1024,1024]{1,0:T(8,128)(2,1)} fusion(bf16[1024,2048]{1,0:T(8,128)(2,1)S(1)} %multiply_convert_fusion, bf16[2048,1024]{1,0:T(8,128)(2,1)S(1)} %copy-done.19), kind=kOutput, calls=%fused_computation.38 | convolution fusion | flops 4296015872 | bytes 10485760 | tf_op jit(solution)/shard_map/dot_general | solution.py:125
  81.9 4.5 %convert_convert_fusion = f32[1024,1024]{1,0:T(8,128)S(1)} fusion(bf16[1024,2048]{1,0:T(8,128)(2,1)S(1)} %multiply_convert_fusion, bf16[2048,1024]{1,0:T(8,128)(2,1)S(1)} %copy-done.20), kind=kOutput, calls=%fused_computation.36 | convolution fusion | flops 4297064448 | bytes 12582912 | tf_op jit(solution)/shard_map/dot_general | solution.py:122
  87.2 1.3 copy-done.6
  88.5 3.0 copy.143
  91.5 3.4 %reduce_sum.89 = f32[1024,8]{1,0:T(8,128)S(1)} reduce(f32[1024,8,128]{2,1,0:T(8,128)} %bitcast.120, f32[]{:T(128)} %constant.162.clone.1), dimensions={2}, to_apply=%region_16.17 | reduce | flops 1040384 | bytes 4227076 | tf_op jit(solution)/shard_map/reduce_sum | solution.py:38
  95.2 2.6 mul.177
  97.8 4.9 %mul.178 = f32[4,2,1,128,1024]{4,3,1,0,2:T(8,128)} reshape(f32[1024,8,128]{2,1,0:T(8,128)} %mul.177) | data formatting | bytes 8388608 | tf_op jit(solution)/shard_map/mul | solution.py:38
  102.7 4.3 %multiply_convert_fusion.2 = bf16[4,2,1,128,1024]{4,3,1,0,2:T(8,128)(2,1)S(1)} fusion(f32[4,2,1,128,1024]{4,3,1,0,2:T(8,128)} %bitcast.119, f32[4,2,1,128,1024]{4,3,1,0,2:T(8,128)} %mul.178), kind=kLoop, calls=%fused_computation.28 | loop fusion | flops 2097152 | bytes 10485760 | tf_op jit(solution)/shard_map/convert_element_type | solution.py:39
  107.2 1.9 collective-permute-start.4
  109.2 5.5 %collective-permute-start.5 = (bf16[1,2,2,128,1024]{4,3,1,0,2:T(8,128)(2,1)S(1)}, bf16[1,2,2,128,1024]{4,3,1,0,2:T(8,128)(2,1)S(1)}, u32[]{:S(2)}, u32[]{:S(2)}) collective-permute-start(bf16[1,2,2,128,1024]{4,3,1,0,2:T(8,128)(2,1)S(1)} %get-tuple-element.221), channel_id=1, source_target_pairs={{16,0},{32,16},{48,32},{64,48},{80,64},{96,80},{112,96},{17,1},{33... | collective-permute-start | bytes 3145736 | tf_op jit(solution)/shard_map/ppermute | solution.py:29
  114.6 20.2 %collective-permute-done.4 = bf16[1,2,2,128,1024]{4,3,1,0,2:T(8,128)(2,1)S(1)} collective-permute-done((bf16[1,2,2,128,1024]{4,3,1,0,2:T(8,128)(2,1)S(1)}, bf16[1,2,2,128,1024]{4,3,1,0,2:T(8,128)(2,1)S(1)}, u32[]{:S(2)}, u32[]{:S(2)}) %collective-permute-start.4) | collective-permute-done | bytes 1048608 | tf_op jit(solution)/shard_map/ppermute | solution.py:27
  134.9 1.8 collective-permute-done.5
  137.7 4.1 %pad_maximum_fusion.1 = bf16[6,2,2,128,1024]{4,3,1,0,2:T(8,128)(2,1)S(1)} fusion(bf16[1,2,2,128,1024]{4,3,1,0,2:T(8,128)(2,1)S(1)} %collective-permute-done.5, bf16[4,2,1,128,1024]{4,3,1,0,2:T(8,128)(2,1)S(1)} %bitcast.117, bf16[4,2,1,128,1024]{4,3,1,0,2:T(8,128)(2,1)S(1)} %multiply_convert_fusion.2, bf16[1,2,2,128,1024]{4,3,1,0,2:T(8,128)(2,1)S(1)} %collective-permute-done.4), kind=kLoop, calls=%fused_computation.21 | loop fusion | flops 9437184 | bytes 12582912 | tf_op jit(solution)/shard_map/concatenate | solution.py:25
  141.8 3.7 %fusion.23 = (bf16[6,1,2,128,1024]{4,3,1,0,2:T(8,128)(2,1)}, bf16[6,1,2,128,1024]{4,3,1,0,2:T(8,128)(2,1)}) fusion(bf16[6,2,2,128,1024]{4,3,1,0,2:T(8,128)(2,1)S(1)} %pad_maximum_fusion.1), kind=kLoop, calls=%fused_computation.99 | loop fusion | bytes 12582912 | tf_op jit(solution)/shard_map/slice | solution.py:24
  145.4 2.7 collective-permute-start.6
  148.2 2.1 collective-permute-start.7
  150.8 8.1 %bitcast_reduce_fusion.1 = (f32[1024,8]{0,1:T(8,128)S(1)}, bf16[1024,1024]{0,1:T(8,128)(2,1)S(1)}) fusion(bf16[1024,2048]{1,0:T(8,128)(2,1)} %copy-done.11, bf16[2048,1024]{1,0:T(8,128)(2,1)} %param.25), kind=kOutput, calls=%fused_computation.25 | convolution fusion | flops 4299153408 | bytes 10518528 | tf_op jit(solution)/shard_map/dot_general | solution.py:118
  159.4 3.0 copy.145
  162.4 5.4 %copy.134 = f32[8,128,8,128]{3,1,2,0:T(8,128)} copy(f32[8,128,8,128]{1,0,3,2:T(8,128)} %bitcast.121) | data formatting | bytes 8388608 | tf_op jit(solution)/shard_map/reshape | solution.py:37
  167.8 4.0 %multiply_convert_fusion.1 = bf16[8,128,8,128]{3,1,2,0:T(8,128)(2,1)} fusion(f32[8,128,8,128]{3,1,2,0:T(8,128)} %copy.134, f32[8,128,8]{1,2,0:T(8,128)S(1)} %rsqrt_bitcast_fusion), kind=kLoop, calls=%fused_computation.27 | loop fusion | flops 2097152 | bytes 6324224 | tf_op jit(solution)/shard_map/convert_element_type | solution.py:39
  171.8 44.6 %collective-permute-done.6 = bf16[6,1,2,128,1024]{4,3,1,0,2:T(8,128)(2,1)} collective-permute-done((bf16[6,1,2,128,1024]{4,3,1,0,2:T(8,128)(2,1)}, bf16[6,1,2,128,1024]{4,3,1,0,2:T(8,128)(2,1)}, u32[]{:S(2)}, u32[]{:S(2)}) %collective-permute-start.6) | collective-permute-done | bytes 3145760 | tf_op jit(solution)/shard_map/ppermute | solution.py:27
  216.4 2.8 collective-permute-done.7
  219.2 6.8 %pad_maximum_fusion = bf16[6,4,2,128,1024]{4,3,1,0,2:T(8,128)(2,1)S(1)} fusion(bf16[6,1,2,128,1024]{4,3,1,0,2:T(8,128)(2,1)} %collective-permute-done.7, bf16[1,2,2,128,1024]{4,3,1,0,2:T(8,128)(2,1)S(1)} %copy-done.10, bf16[4,2,1,128,1024]{4,3,1,0,2:T(8,128)(2,1)S(1)} %bitcast.118, bf16[4,2,1,128,1024]{4,3,1,0,2:T(8,128)(2,1)S(1)} %multiply_convert_fusion.2, ...), kind=kLoop, calls=%fused_computation.17 | loop fusion | flops 31457280 | bytes 25165824 | tf_op jit(solution)/shard_map/concatenate | solution.py:25
  225.9 2.9 copy.144
  228.8 5.1 %copy.142 = bf16[24,2,128,8,128]{4,3,2,1,0:T(8,128)(2,1)} copy(bf16[24,2,128,8,128]{4,3,2,0,1:T(8,128)(2,1)S(1)} %bitcast.115) | data formatting | bytes 25165824 | tf_op jit(solution)/shard_map/reshape | solution.py:140
  233.9 66.3 %while.16 = (s32[]{:T(128)}, f32[8,128,8,128]{1,3,2,0:T(8,128)}, f32[8,8,128]{2,1,0:T(8,128)S(1)}, s32[8,4]{0,1:T(4,128)S(1)}, bf16[24,2,128,8,128]{4,3,2,1,0:T(...) while((s32[]{:T(128)}, f32[8,128,8,128]{1,3,2,0:T(8,128)}, ...), condition=%wide.region_20.21_spmd.clone, body=%wide.region_18.20_spmd.clone.sunk | while | flops 547365952 | bytes 73537904 | solution.py:180
  234.0 7.6 %gather_fusion = bf16[8,2,128,8,128]{4,3,2,1,0:T(8,128)(2,1)} fusion(bf16[24,2,128,8,128]{4,3,2,1,0:T(8,128)(2,1)} %get-tuple-element.319, s32[1024]{0:T(1024)S(1)} %pad_clamp_fusion.2), kind=kCustom, calls=%fused_computation.clone.clone.1 | custom fusion | bytes 8388640 | tf_op jit(solution)/shard_map/while/body/eval_jaxpr/jit(_take)/gather | solution.py:155
  241.6 2.8 copy_select_fusion.2
  244.4 1.6 bitcast_reduce_fusion.3
  246.6 2.0 bitcast_add_fusion.2
  248.6 1.9 copy-done.3
  250.6 7.6 %gather_fusion = bf16[8,2,128,8,128]{4,3,2,1,0:T(8,128)(2,1)} fusion(bf16[24,2,128,8,128]{4,3,2,1,0:T(8,128)(2,1)} %get-tuple-element.319, s32[1024]{0:T(1024)S(1)} %pad_clamp_fusion.2), kind=kCustom, calls=%fused_computation.clone.clone.1 | custom fusion | bytes 8388640 | tf_op jit(solution)/shard_map/while/body/eval_jaxpr/jit(_take)/gather | solution.py:155
  258.2 2.8 copy_select_fusion.2
  260.9 1.6 bitcast_reduce_fusion.3
  263.1 2.0 bitcast_add_fusion.2
  265.2 1.9 copy-done.3
  267.1 7.6 %gather_fusion = bf16[8,2,128,8,128]{4,3,2,1,0:T(8,128)(2,1)} fusion(bf16[24,2,128,8,128]{4,3,2,1,0:T(8,128)(2,1)} %get-tuple-element.319, s32[1024]{0:T(1024)S(1)} %pad_clamp_fusion.2), kind=kCustom, calls=%fused_computation.clone.clone.1 | custom fusion | bytes 8388640 | tf_op jit(solution)/shard_map/while/body/eval_jaxpr/jit(_take)/gather | solution.py:155
  274.7 2.8 copy_select_fusion.2
  277.5 1.6 bitcast_reduce_fusion.3
  279.7 2.0 bitcast_add_fusion.2
  281.7 1.9 copy-done.3
  283.7 7.6 %gather_fusion = bf16[8,2,128,8,128]{4,3,2,1,0:T(8,128)(2,1)} fusion(bf16[24,2,128,8,128]{4,3,2,1,0:T(8,128)(2,1)} %get-tuple-element.319, s32[1024]{0:T(1024)S(1)} %pad_clamp_fusion.2), kind=kCustom, calls=%fused_computation.clone.clone.1 | custom fusion | bytes 8388640 | tf_op jit(solution)/shard_map/while/body/eval_jaxpr/jit(_take)/gather | solution.py:155
  291.3 2.8 copy_select_fusion.2
  294.1 1.6 bitcast_reduce_fusion.3
  296.2 2.0 bitcast_add_fusion.2
  298.3 1.9 copy-done.3
  300.2 2.8 divide_convert_fusion
  303.0 2.8 copy.135
  305.8 4.2 %reshape.240 = bf16[4,4,64,1024]{3,2,1,0:T(8,128)(2,1)} reshape(bf16[8,128,8,128]{3,2,1,0:T(8,128)(2,1)} %copy.135) | data formatting | bytes 4194304 | tf_op jit(solution)/shard_map/reshape | solution.py:184
  (136 shorter events, 16.0 us)
Async XLA Ops:
  0.0 63.8 %copy-start = (bf16[16,3,3,3,512]{4,0,3,2,1:T(8,128)(2,1)S(1)}, bf16[16,3,3,3,512]{4,0,3,2,1:T(8,128)(2,1)}, u32[]{:S(2)}) copy-start(bf16[16,3,3,3,512]{4,0,3,2,1:T(8,128)(2,1)} %param.19) | copy-start | bytes 1327108
  0.0 53.2 %copy-start.17 = (f32[512]{0:T(512)S(1)}, f32[512]{0:T(512)}, u32[]{:S(2)}) copy-start(f32[512]{0:T(512)} %param.18) | copy-start | bytes 6148
  0.0 53.2 %copy-start.16 = (f32[512]{0:T(512)S(1)}, f32[512]{0:T(512)}, u32[]{:S(2)}) copy-start(f32[512]{0:T(512)} %param.17) | copy-start | bytes 6148
  1.1 45.5 %collective-permute-start.1 = (bf16[1,4,64,512]{3,2,1,0:T(8,128)(2,1)S(1)}, bf16[1,4,64,512]{3,2,1,0:T(8,128)(2,1)S(1)}, u32[]{:S(2)}, u32[]{:S(2)}) collective-permute-start(bf16[1,4,64,512]{3,2,1,0:T(8,128)(2,1)S(1)} %get-tuple-element.224), channel_id=1, source_target_pairs={{16,0},{32,16},{48,32},{64,48},{80,64},{96,80},{112,96},{17,1},{33... | collective-permute-start | bytes 786440 | tf_op jit(solution)/shard_map/ppermute | solution.py:29
  6.7 38.6 %collective-permute-start = (bf16[1,4,64,512]{3,2,1,0:T(8,128)(2,1)S(1)}, bf16[1,4,64,512]{3,2,1,0:T(8,128)(2,1)S(1)}, u32[]{:S(2)}, u32[]{:S(2)}) collective-permute-start(bf16[1,4,64,512]{3,2,1,0:T(8,128)(2,1)S(1)} %get-tuple-element.225), channel_id=1, source_target_pairs={{0,16},{16,32},{32,48},{48,64},{64,80},{80,96},{96,112},{1,17},{17... | collective-permute-start | bytes 786440 | tf_op jit(solution)/shard_map/ppermute | solution.py:27
  46.8 9.2 %collective-permute-start.2 = (bf16[6,1,64,512]{3,2,1,0:T(8,128)(2,1)S(1)}, bf16[6,1,64,512]{3,2,1,0:T(8,128)(2,1)S(1)}, u32[]{:S(2)}, u32[]{:S(2)}) collective-permute-start(bf16[6,1,64,512]{3,2,1,0:T(8,128)(2,1)S(1)} %get-tuple-element.222), channel_id=1, source_target_pairs={{0,1},{1,2},{2,3},{3,4},{4,5},{5,6},{6,7},{7,8},{8,9},{9,10},{10,1... | collective-permute-start | bytes 1179656 | tf_op jit(solution)/shard_map/ppermute | solution.py:27
  51.2 11.0 %collective-permute-start.3 = (bf16[6,1,64,512]{3,2,1,0:T(8,128)(2,1)S(1)}, bf16[6,1,64,512]{3,2,1,0:T(8,128)(2,1)S(1)}, u32[]{:S(2)}, u32[]{:S(2)}) collective-permute-start(bf16[6,1,64,512]{3,2,1,0:T(8,128)(2,1)S(1)} %get-tuple-element.223), channel_id=1, source_target_pairs={{1,0},{2,1},{3,2},{4,3},{5,4},{6,5},{7,6},{8,7},{9,8},{10,9},{11,1... | collective-permute-start | bytes 1179656 | tf_op jit(solution)/shard_map/ppermute | solution.py:29
  66.5 2.7 copy-start.13
  66.5 2.7 copy-start.15
  66.5 2.7 copy-start.18
  74.0 2.2 copy-start.19
  76.2 5.7 %copy-start.11 = (bf16[1024,2048]{1,0:T(8,128)(2,1)}, bf16[1024,2048]{1,0:T(8,128)(2,1)S(1)}, u32[]{:S(2)}) copy-start(bf16[1024,2048]{1,0:T(8,128)(2,1)S(1)} %multiply_convert_fusion) | copy-start | bytes 12582916
  76.2 5.7 %copy-start.20 = (bf16[2048,1024]{1,0:T(8,128)(2,1)S(1)}, bf16[2048,1024]{1,0:T(8,128)(2,1)}, u32[]{:S(2)}) copy-start(bf16[2048,1024]{1,0:T(8,128)(2,1)} %param.26) | copy-start | bytes 12582916
  86.3 2.1 copy-start.6
  102.7 4.3 %copy-start.4 = (bf16[1024,1024]{1,0:T(8,128)(2,1)S(1)}, bf16[1024,1024]{1,0:T(8,128)(2,1)}, u32[]{:S(2)}) copy-start(bf16[1024,1024]{1,0:T(8,128)(2,1)} %convolution_convert_fusion.1) | copy-start | bytes 6291460
  107.2 27.6 %collective-permute-start.4 = (bf16[1,2,2,128,1024]{4,3,1,0,2:T(8,128)(2,1)S(1)}, bf16[1,2,2,128,1024]{4,3,1,0,2:T(8,128)(2,1)S(1)}, u32[]{:S(2)}, u32[]{:S(2)}) collective-permute-start(bf16[1,2,2,128,1024]{4,3,1,0,2:T(8,128)(2,1)S(1)} %get-tuple-element.220), channel_id=1, source_target_pairs={{0,16},{16,32},{32,48},{48,64},{64,80},{80,96},{96,112},{1,17},{17... | collective-permute-start | bytes 3145736 | tf_op jit(solution)/shard_map/ppermute | solution.py:27
  109.2 27.5 %collective-permute-start.5 = (bf16[1,2,2,128,1024]{4,3,1,0,2:T(8,128)(2,1)S(1)}, bf16[1,2,2,128,1024]{4,3,1,0,2:T(8,128)(2,1)S(1)}, u32[]{:S(2)}, u32[]{:S(2)}) collective-permute-start(bf16[1,2,2,128,1024]{4,3,1,0,2:T(8,128)(2,1)S(1)} %get-tuple-element.221), channel_id=1, source_target_pairs={{16,0},{32,16},{48,32},{64,48},{80,64},{96,80},{112,96},{17,1},{33... | collective-permute-start | bytes 3145736 | tf_op jit(solution)/shard_map/ppermute | solution.py:29
  134.9 1.8 copy-start.7
  136.6 1.1 copy-start.9
  141.8 8.6 %copy-start.14 = (s32[4,2,4]{2,1,0:T(2,128)S(1)}, s32[4,2,4]{2,1,0:T(2,128)}, u32[]{:S(2)}) copy-start(s32[4,2,4]{2,1,0:T(2,128)} %param.29) | copy-start | bytes 388
  141.8 9.0 %copy-start.21 = (f32[8]{0:T(128)S(1)}, f32[8]{0:T(128)}, u32[]{:S(2)}) copy-start(f32[8]{0:T(128)} %param.28) | copy-start | bytes 100
  145.4 70.9 %collective-permute-start.6 = (bf16[6,1,2,128,1024]{4,3,1,0,2:T(8,128)(2,1)}, bf16[6,1,2,128,1024]{4,3,1,0,2:T(8,128)(2,1)}, u32[]{:S(2)}, u32[]{:S(2)}) collective-permute-start(bf16[6,1,2,128,1024]{4,3,1,0,2:T(8,128)(2,1)} %get-tuple-element.218), channel_id=1, source_target_pairs={{0,1},{1,2},{2,3},{3,4},{4,5},{5,6},{6,7},{7,8},{8,9},{9,10},{10,1... | collective-permute-start | bytes 9437192 | tf_op jit(solution)/shard_map/ppermute | solution.py:27
  148.2 71.0 %collective-permute-start.7 = (bf16[6,1,2,128,1024]{4,3,1,0,2:T(8,128)(2,1)}, bf16[6,1,2,128,1024]{4,3,1,0,2:T(8,128)(2,1)}, u32[]{:S(2)}, u32[]{:S(2)}) collective-permute-start(bf16[6,1,2,128,1024]{4,3,1,0,2:T(8,128)(2,1)} %get-tuple-element.219), channel_id=1, source_target_pairs={{1,0},{2,1},{3,2},{4,3},{5,4},{6,5},{7,6},{8,7},{9,8},{10,9},{11,1... | collective-permute-start | bytes 9437192 | tf_op jit(solution)/shard_map/ppermute | solution.py:29
  167.8 51.4 %copy-start.5 = (bf16[1024,1024]{1,0:T(8,128)(2,1)S(1)}, bf16[1024,1024]{1,0:T(8,128)(2,1)}, u32[]{:S(2)}) copy-start(bf16[1024,1024]{1,0:T(8,128)(2,1)} %convolution_convert_fusion.1) | copy-start | bytes 6291460
  167.8 51.4 %copy-start.8 = (bf16[1,2,2,128,1024]{4,3,1,0,2:T(8,128)(2,1)S(1)}, bf16[1,2,2,128,1024]{4,3,1,0,2:T(8,128)(2,1)}, u32[]{:S(2)}) copy-start(bf16[1,2,2,128,1024]{4,3,1,0,2:T(8,128)(2,1)} %copy-done.7) | copy-start | bytes 3145732
  167.8 51.4 %copy-start.10 = (bf16[1,2,2,128,1024]{4,3,1,0,2:T(8,128)(2,1)S(1)}, bf16[1,2,2,128,1024]{4,3,1,0,2:T(8,128)(2,1)}, u32[]{:S(2)}) copy-start(bf16[1,2,2,128,1024]{4,3,1,0,2:T(8,128)(2,1)} %copy-done.9) | copy-start | bytes 3145732
  228.8 5.1 %copy-start.12 = (bf16[8,128,8,128]{3,1,2,0:T(8,128)(2,1)S(1)}, bf16[8,128,8,128]{3,1,2,0:T(8,128)(2,1)}, u32[]{:S(2)}) copy-start(bf16[8,128,8,128]{3,1,2,0:T(8,128)(2,1)} %multiply_convert_fusion.1) | copy-start | bytes 6291460
  244.4 2.2 copy-start.2
  248.6 1.9 copy-start.3
  260.9 2.2 copy-start.2
  265.1 1.9 copy-start.3
  277.5 2.2 copy-start.2
  281.7 1.9 copy-start.3
  294.1 2.2 copy-start.2
  298.3 1.9 copy-start.3
  300.2 9.8 %copy-start.1 = (bf16[16,3,3,3,512]{4,0,3,2,1:T(8,128)(2,1)S(1)}, bf16[16,3,3,3,512]{4,0,3,2,1:T(8,128)(2,1)}, u32[]{:S(2)}) copy-start(bf16[16,3,3,3,512]{4,0,3,2,1:T(8,128)(2,1)} %param.19) | copy-start | bytes 1327108
where the time goes:
time: 313 us; the launch traced here: 310 us
  local copies, waits for them, and re-layouts  87.6 us (28%)
  waiting for transfers between devices  78.3 us (25%)
  other arithmetic  44.8 us (14%)
  matrix products  38.8 us (12%)
  blocking collectives  33.6 us (11%)
  starting transfers between devices  26.1 us (8%)
    ppermute x4, waiting for transfers between devices, with_halo(): lax.ppermute(tail, axis, [(i, (i + 1) % count) for i in range(ends)])  67.5 us
    psum x5, blocking collectives, by_axis(): shard = lax.psum(shard, axis)  33.6 us
    gather x4, local copies, waits for them, and re-layouts, attend_slot(): jnp.take(nearby, lax.dynamic_index_in_dim(where_local, slot_index, 1, kee...  30.4 us
    ppermute x4, starting transfers between devices, with_halo(): lax.ppermute(head, axis, [((i + 1) % count, i) for i in range(ends)])  15.1 us
    unnamed x45, local copies, waits for them, and re-layouts  13.7 us
    select_n x4, other arithmetic, attend_slot(): jnp.take(nearby, lax.dynamic_index_in_dim(where_local, slot_index, 1, kee...  11.1 us
    ppermute x4, starting transfers between devices, with_halo(): lax.ppermute(tail, axis, [(i, (i + 1) % count) for i in range(ends)])  11 us
    ppermute x4, waiting for transfers between devices, with_halo(): lax.ppermute(head, axis, [((i + 1) % count, i) for i in range(ends)])  10.8 us
  transfers between devices with their start and end apart: 8, of which 6 were waited for; matrix products, arithmetic and copies ran while one was open for 8% of the time, Pallas kernels for 0%

commit v1 on v0

v1 whole, which is shorter than its diff:
```python
import functools

import jax
import jax.numpy as jnp
from jax import lax
from jax.experimental import pallas as pl
from jax.experimental.pallas import tpu as pltpu
from jax.sharding import PartitionSpec as P

MESH = pl.DeviceIdType.MESH
F32, BF16 = jnp.float32, jnp.bfloat16
GROUP = 16
NT_DIMS = (((1,), (1,)), ((), ()))
TN_DIMS = (((0,), (0,)), ((), ()))
MIB = 1 << 20


def remote(src, dst, send, recv, tm, row):
    return pltpu.make_async_remote_copy(
        src_ref=src,
        dst_ref=dst,
        send_sem=send,
        recv_sem=recv,
        device_id={"tm": tm, "row": row},
        device_id_type=MESH,
    )


def group_sum(x):
    lane = lax.broadcasted_iota(jnp.int32, x.shape, 1)
    for k in (1, 2, 4, 8):
        down = pltpu.roll(x, 128 - k, 1)
        up = pltpu.roll(x, k, 1)
        x = x + jnp.where((lane & k) == 0, down, up)
    return x


def mask_rows(mask_token):
    hi = mask_token.astype(BF16).astype(F32)
    mid = (mask_token - hi).astype(BF16).astype(F32)
    low = mask_token - hi - mid
    row = lax.broadcasted_iota(jnp.int32, (16, mask_token.shape[1]), 0)
    zero = jnp.zeros(row.shape, F32)
    return jnp.where(row == 0, hi, jnp.where(row == 1, mid, jnp.where(row == 2, low, zero))).astype(BF16)


def layer_norm(tokens, pos):
    x = tokens + pos.astype(F32)
    c = x - jnp.mean(x, axis=-1, keepdims=True)
    return (c * lax.rsqrt(jnp.mean(c * c, axis=-1, keepdims=True) + 1e-05)).astype(BF16)


def head_norm(y):
    y = y.astype(BF16).astype(F32)
    parts = []
    for i in range(y.shape[1] // 128):
        part = y[:, 128 * i : 128 * (i + 1)]
        parts.append(part * lax.rsqrt(jnp.mean(part * part, axis=-1, keepdims=True) + 1e-06))
    return jnp.concatenate(parts, axis=1).astype(BF16)


def front(
    tm_n, row_n,
    feat, aux, taps, embed, mask_token, pos, wq, wk, wv,
    q_out, k_out, v_out, pos_halo, lat_halo,
    cells, act, aux_v, taps_v, emb_v, mtok_v, pos_v, w_v, hidden, tok, lat, qkv, mine, stat_r, stat_t, affine,
    load, f_send, f_recv, r_send, r_recv, t_send, t_recv, p_send, p_recv, c_send, c_recv, l_send, l_recv,
):
    tm, row = lax.axis_index("tm"), lax.axis_index("row")

    def wrap(i, n):
        return lax.rem(i + n, n)

    before, after = wrap(tm - 1, tm_n), wrap(tm + 1, tm_n)
    above, below = wrap(row - 1, row_n), wrap(row + 1, row_n)

    own = pltpu.make_async_copy(feat, cells.at[1:5, 1:5], load.at[0])
    own.start()
    local = [
        pltpu.make_async_copy(aux, aux_v, load.at[1]),
        pltpu.make_async_copy(taps, taps_v, load.at[2]),
        pltpu.make_async_copy(embed, emb_v.at[0:16], load.at[3]),
        pltpu.make_async_copy(mask_token, mtok_v, load.at[4]),
        pltpu.make_async_copy(pos, pos_v, load.at[5]),
        pltpu.make_async_copy(wq, w_v.at[0], load.at[6]),
        pltpu.make_async_copy(wk, w_v.at[1], load.at[7]),
        pltpu.make_async_copy(wv, w_v.at[2], load.at[8]),
    ]
    for copy in local:
        copy.start()

    barrier = pltpu.get_barrier_semaphore()
    for d in range(1, row_n):
        pl.semaphore_signal(barrier, inc=1, device_id={"tm": tm, "row": wrap(row + d, row_n)}, device_id_type=MESH)
    for d in range(1, tm_n):
        pl.semaphore_signal(barrier, inc=1, device_id={"tm": wrap(tm + d, tm_n), "row": row}, device_id_type=MESH)
    for t in (before, after):
        for r in (above, below):
            pl.semaphore_signal(barrier, inc=1, device_id={"tm": t, "row": r}, device_id_type=MESH)
    pl.semaphore_wait(barrier, row_n - 1 + tm_n - 1 + 4)

    halo = [
        (feat.at[:, 3], cells.at[1:5, 0], tm, below),
        (feat.at[:, 0], cells.at[1:5, 5], tm, above),
        (feat.at[3], cells.at[0, 1:5], after, row),
        (feat.at[0], cells.at[5, 1:5], before, row),
        (feat.at[3, 3], cells.at[0, 0], after, below),
        (feat.at[3, 0], cells.at[0, 5], after, above),
        (feat.at[0, 3], cells.at[5, 0], before, below),
        (feat.at[0, 0], cells.at[5, 5], before, above),
    ]
    feat_copies = [
        remote(src, dst, f_send.at[i], f_recv.at[i], t, r) for i, (src, dst, t, r) in enumerate(halo)
    ]
    for copy in feat_copies:
        copy.start()

    own.wait()
    half = jnp.zeros((8, 512), F32)

    def add_row(i, carry):
        total, square = carry
        x = cells[1 + i // 4, 1 + i % 4].astype(F32)
        for j in range(8):
            part = x[8 * j : 8 * (j + 1)]
            total, square = total + part, square + part * part
        return total, square

    total, square = lax.fori_loop(0, 16, add_row, (half, half))
    total = jnp.sum(total, axis=0, keepdims=True)
    square = jnp.sum(square, axis=0, keepdims=True)
    for i in range(4):
        mine[0, i : i + 1] = total[:, 128 * i : 128 * (i + 1)]
        mine[0, 4 + i : 5 + i] = square[:, 128 * i : 128 * (i + 1)]
    row_copies = [
        remote(mine.at[0], stat_r.at[d - 1], r_send.at[d - 1], r_recv.at[d - 1], tm, wrap(row + d, row_n))
        for d in range(1, row_n)
    ]
    for copy in row_copies:
        copy.start()
    for copy in row_copies:
        copy.wait_recv()
    mine[1] = mine[0] + jnp.sum(stat_r[...], axis=0)
    tm_copies = [
        remote(mine.at[1], stat_t.at[d - 1], t_send.at[d - 1], t_recv.at[d - 1], wrap(tm + d, tm_n), row)
        for d in range(1, tm_n)
    ]
    for copy in tm_copies:
        copy.start()
    for copy in tm_copies:
        copy.wait_recv()

    pos_copies = {}
    for i, t in enumerate((0, 3, 1, 2)):
        pos_copies["down", t] = remote(pos.at[2 * t + 1], pos_halo.at[1 + t, 0], p_send.at[i], p_recv.at[i], tm, below)
        pos_copies["up", t] = remote(pos.at[2 * t], pos_halo.at[1 + t, 3], p_send.at[4 + i], p_recv.at[4 + i], tm, above)
    pos_copies["after", 0] = remote(pos.at[6:8], pos_halo.at[0, 1:3], p_send.at[8], p_recv.at[8], after, row)
    pos_copies["before", 0] = remote(pos.at[0:2], pos_halo.at[5, 1:3], p_send.at[9], p_recv.at[9], before, row)
    for copy in pos_copies.values():
        copy.start()

    for copy in local[:5]:
        copy.wait()
    every = group_sum(mine[1] + jnp.sum(stat_t[...], axis=0))
    count = tm_n * row_n * 4 * 4 * 64 * GROUP
    average = every[0:4] / count
    variance = every[4:8] / count - average * average
    inverse = lax.rsqrt(variance + 1e-06)
    affine[0:4] = inverse * aux_v[0:4]
    affine[4:8] = aux_v[4:8] - average * inverse * aux_v[0:4]
    emb_v[16:32] = mask_rows(mtok_v[...])

    for copy in feat_copies:
        copy.wait_recv()

    def activate(i, _):
        f, r = i // 6, i % 6
        frame, line = tm * 4 + f - 1, row * 4 + r - 1
        inside = (frame >= 0) & (frame < tm_n * 4) & (line >= 0) & (line < row_n * 4)
        keep = jnp.where(inside, 0.5, 0.0)
        for j in range(4):
            lanes = slice(128 * j, 128 * (j + 1))
            v = cells[f, r, :, lanes].astype(F32) * affine[j : j + 1] + affine[4 + j : 5 + j]
            v = (v * keep) * (1.0 + jnp.tanh(0.5 * v))
            act[f, pl.ds(pl.multiple_of(r * 64, 64), 64), lanes] = v.astype(BF16)
        return 0

    lax.fori_loop(0, 36, activate, 0)

    column = lax.broadcasted_iota(jnp.int32, (16, 256), 1) % 64
    third = lax.broadcasted_iota(jnp.int32, (16, 128), 0) < 3

    def convolve(t, _):
        acc = jnp.zeros((144, 384), F32)
        for a in range(3):
            acc = acc + lax.dot_general(taps_v[a], act[t + a], NT_DIMS, preferred_element_type=F32)
        sums = []
        for c in range(3):
            part = acc[16 * c : 16 * c + 16]
            for b in (1, 2):
                part = part + pltpu.roll(acc[48 * b + 16 * c : 48 * b + 16 * c + 16], 384 - 64 * b, 1)
            sums.append(part[:, :256])
        left = jnp.where(column == 0, 0.0, pltpu.roll(sums[0], 1, 1))
        right = jnp.where(column == 63, 0.0, pltpu.roll(sums[2], 255, 1))
        out = sums[1] + left + right
        for p in range(2):
            masked = aux_v[pl.ds(24 + 2 * t + p, 1)]
            value = (out[:, 128 * p : 128 * (p + 1)] + aux_v[8:24]).astype(BF16).astype(F32)
            lat[2 * t + p, 0:16] = jnp.where(masked > 0.5, 0.0, value).astype(BF16)
            lat[2 * t + p, 16:32] = jnp.where(third, masked, 0.0).astype(BF16)
        return 0

    lax.fori_loop(0, 4, convolve, 0)

    lat_sends = []
    for t in range(4):
        lat_sends.append((lat.at[2 * t + 1], lat_halo.at[1 + t, 0], tm, below))
        lat_sends.append((lat.at[2 * t], lat_halo.at[1 + t, 3], tm, above))
    lat_sends += [
        (lat.at[6:8], lat_halo.at[0, 1:3], after, row),
        (lat.at[0:2], lat_halo.at[5, 1:3], before, row),
        (lat.at[7], lat_halo.at[0, 0], after, below),
        (lat.at[6], lat_halo.at[0, 3], after, above),
        (lat.at[1], lat_halo.at[5, 0], before, below),
        (lat.at[0], lat_halo.at[5, 3], before, above),
    ]
    lat_copies = [remote(src, dst, l_send.at[i], l_recv.at[i], t, r) for i, (src, dst, t, r) in enumerate(lat_sends)]
    for copy in lat_copies:
        copy.start()

    def normalize(j, _):
        tok[...] = lax.dot_general(lat[j], emb_v[...], TN_DIMS, preferred_element_type=F32)

        def piece(i, _):
            rows = pl.ds(pl.multiple_of(i * 16, 16), 16)
            hidden[pl.ds(pl.multiple_of(j * 128 + i * 16, 16), 16)] = layer_norm(tok[rows], pos_v[j, rows])
            return 0

        lax.fori_loop(0, 8, piece, 0)
        return 0

    lax.fori_loop(0, 8, normalize, 0)

    def project(n, normed):
        def tile(i, _):
            m, c = i // 4, i % 4
            columns = pl.ds(pl.multiple_of(c * 256, 256), 256)
            y = jnp.dot(
                hidden[pl.ds(pl.multiple_of(m * 512, 512), 512)], w_v[n, :, columns], preferred_element_type=F32
            )
            y = head_norm(y) if normed else y.astype(BF16)
            qkv[n, pl.ds(m * 4, 4), :, columns] = y.reshape(4, 128, 256)
            return 0

        lax.fori_loop(0, 8, tile, 0)

    stores = [pltpu.make_async_copy(qkv.at[n], out, load.at[9 + n]) for n, out in enumerate((q_out, k_out, v_out))]
    local[5].wait()
    project(0, True)
    stores[0].start()

    odd = lax.rem(row, 2)
    other = row + 1 - 2 * odd
    outer = 3 * odd
    inner_src = 2 - odd
    for t in (0, 3):
        pos_copies["down", t].wait_recv()
        pos_copies["up", t].wait_recv()
    pos_copies["after", 0].wait_recv()
    pos_copies["before", 0].wait_recv()
    corner = [
        remote(pos_halo.at[1, outer], pos_halo.at[5, outer], c_send.at[0], c_recv.at[0], before, row),
        remote(pos_halo.at[4, outer], pos_halo.at[0, outer], c_send.at[1], c_recv.at[1], after, row),
        remote(pos_halo.at[0, inner_src], pos_halo.at[0, outer], c_send.at[2], c_recv.at[2], tm, other),
        remote(pos_halo.at[5, inner_src], pos_halo.at[5, outer], c_send.at[3], c_recv.at[3], tm, other),
    ]
    for copy in corner:
        copy.start()

    local[6].wait()
    project(1, True)
    stores[1].start()
    local[7].wait()
    project(2, False)
    stores[2].start()

    for t in (1, 2):
        pos_copies["down", t].wait_recv()
        pos_copies["up", t].wait_recv()
    for copy in [*lat_copies, *corner]:
        copy.wait_recv()
    for copy in [*feat_copies, *row_copies, *tm_copies, *pos_copies.values(), *lat_copies, *corner]:
        copy.wait_send()
    for copy in stores:
        copy.wait()


def back(
    tm_n, row_n,
    pattern, scale, q, k, v, pos_halo, lat_halo, embed, mask_token, wk, wv,
    out,
    place, need, q_v, k_v, v_v, lat_v, emb_v, mtok_v, w_v, pos_v, tok, hidden, out_v,
    load, p_sem, o_sem,
):
    tm, row = lax.axis_index("tm"), lax.axis_index("row")
    copies = [
        pltpu.make_async_copy(lat_halo, lat_v, load.at[0]),
        pltpu.make_async_copy(embed, emb_v.at[0:16], load.at[1]),
        pltpu.make_async_copy(mask_token, mtok_v, load.at[2]),
        pltpu.make_async_copy(wk, w_v.at[0], load.at[3]),
        pltpu.make_async_copy(wv, w_v.at[1], load.at[4]),
        pltpu.make_async_copy(q, q_v, load.at[5]),
    ]
    for t in range(4):
        copies.append(pltpu.make_async_copy(k.at[2 * t : 2 * t + 2], k_v.at[4 * t + 5 : 4 * t + 7], load.at[6 + t]))
        copies.append(pltpu.make_async_copy(v.at[2 * t : 2 * t + 2], v_v.at[4 * t + 5 : 4 * t + 7], load.at[10 + t]))
    for copy in copies:
        copy.start()

    def clear(i, _):
        need[i] = 0
        return 0

    lax.fori_loop(0, 24, clear, 0)

    def visit(i, _):
        b, s = i // 4, i % 4
        block = pattern[b, s]
        spot = ((block // (2 * row_n)) - tm * 4 + 1) * 4 + (block % (2 * row_n)) - row * 2 + 1
        spot = jnp.where(block >= 0, spot, 5)
        place[i] = spot
        need[spot] = 1
        return 0

    lax.fori_loop(0, 32, visit, 0)

    def gather(i, n):
        f, p = i // 4, i % 4
        own = (f >= 1) & (f <= 4) & (p >= 1) & (p <= 2)
        wanted = (need[i] == 1) & jnp.logical_not(own)

        @pl.when(wanted)
        def _():
            need[24 + n] = i
            pltpu.make_async_copy(pos_halo.at[f, p], pos_v.at[n], p_sem.at[n]).start()

        return n + jnp.where(wanted, 1, 0)

    n = lax.fori_loop(0, 24, gather, 0)

    for copy in copies[:5]:
        copy.wait()
    emb_v[16:32] = mask_rows(mtok_v[...])

    def pair(g, _):
        for u in range(2):
            i = 2 * g + u
            at = jnp.minimum(i, n - 1)
            spot = need[24 + at]

            @pl.when(i < n)
            def _():
                pltpu.make_async_copy(pos_halo.at[0, 0], pos_v.at[at], p_sem.at[at]).wait()

            tok[...] = lax.dot_general(lat_v[spot // 4, spot % 4], emb_v[...], TN_DIMS, preferred_element_type=F32)

            def piece(c, _):
                rows = pl.ds(pl.multiple_of(c * 16, 16), 16)
                hidden[pl.ds(pl.multiple_of(u * 128 + c * 16, 16), 16)] = layer_norm(tok[rows], pos_v[at, rows])
                return 0

            lax.fori_loop(0, 8, piece, 0)
        first = need[24 + 2 * g]
        second = need[24 + jnp.minimum(2 * g + 1, n - 1)]

        def tile(c, _):
            columns = pl.ds(pl.multiple_of(c * 256, 256), 256)
            y = head_norm(jnp.dot(hidden[...], w_v[0, :, columns], preferred_element_type=F32))
            k_v[first, :, columns] = y[0:128]
            k_v[second, :, columns] = y[128:256]
            y = jnp.dot(hidden[...], w_v[1, :, columns], preferred_element_type=F32).astype(BF16)
            v_v[first, :, columns] = y[0:128]
            v_v[second, :, columns] = y[128:256]
            return 0

        lax.fori_loop(0, 4, tile, 0)
        return 0

    lax.fori_loop(0, (n + 1) // 2, pair, 0)
    for copy in copies[5:]:
        copy.wait()

    def attend(b, live):
        spots = [place[4 * b + s] for s in range(live)]

        def head(h, _):
            columns = pl.ds(pl.multiple_of(h * 128, 128), 128)
            query = q_v[b, :, columns]
            factor = scale[h] / 128.0
            total = acc = None
            for spot in spots:
                score = lax.dot_general(query, k_v[spot, :, columns], NT_DIMS, preferred_element_type=F32)
                weight = jnp.exp(score * factor)
                part = jnp.dot(weight.astype(BF16), v_v[spot, :, columns], preferred_element_type=F32)
                total = weight if total is None else total + weight
                acc = part if acc is None else acc + part
            out_v[b, :, columns] = (acc / jnp.sum(total, axis=-1, keepdims=True)).astype(BF16)
            return 0

        lax.fori_loop(0, 8, head, 0, unroll=4)

    def block(b, _):
        live = sum((pattern[b, s] >= 0).astype(jnp.int32) for s in range(4))
        for count in range(1, 5):
            pl.when(live == count)(functools.partial(attend, b, count))
        pltpu.make_async_copy(out_v.at[b], out.at[b], o_sem.at[b]).start()
        return 0

    lax.fori_loop(0, 8, block, 0)
    for b in range(8):
        pltpu.make_async_copy(out_v.at[b], out.at[b], o_sem.at[b]).wait()


def per_device(
    tm_n, row_n,
    features, norm_gain, norm_bias, latent_kernel, latent_bias, token_mask, embed_weight, mask_token, pos_embed,
    query_weight, key_weight, value_weight, logit_scale, pattern,
):
    taps = latent_kernel.transpose(1, 2, 3, 0, 4).reshape(3, 144, 512)
    aux = jnp.concatenate(
        [
            norm_gain.reshape(4, 128),
            norm_bias.reshape(4, 128),
            jnp.broadcast_to(latent_bias[:, None], (16, 128)),
            token_mask.reshape(8, 128).astype(F32),
        ]
    )
    pos = pos_embed.reshape(8, 128, 2048)
    mtok = mask_token.reshape(1, 2048)
    anywhere = pl.BlockSpec(memory_space=pl.ANY)
    dma = pltpu.SemaphoreType.DMA
    block = jax.ShapeDtypeStruct((8, 128, 1024), BF16)
    q, k, v, pos_halo, lat_halo = pl.pallas_call(
        functools.partial(front, tm_n, row_n),
        name="front",
        out_shape=[
            block, block, block,
            jax.ShapeDtypeStruct((6, 4, 128, 2048), BF16),
            jax.ShapeDtypeStruct((6, 4, 32, 128), BF16),
        ],
        in_specs=[anywhere] * 9,
        out_specs=[anywhere] * 5,
        scratch_shapes=[
            pltpu.VMEM((6, 6, 64, 512), BF16),
            pltpu.VMEM((6, 384, 512), BF16),
            pltpu.VMEM((32, 128), F32),
            pltpu.VMEM((3, 144, 512), BF16),
            pltpu.VMEM((32, 2048), BF16),
            pltpu.VMEM((1, 2048), F32),
            pltpu.VMEM((8, 128, 2048), BF16),
            pltpu.VMEM((3, 2048, 1024), BF16),
            pltpu.VMEM((1024, 2048), BF16),
            pltpu.VMEM((128, 2048), F32),
            pltpu.VMEM((8, 32, 128), BF16),
            pltpu.VMEM((3, 8, 128, 1024), BF16),
            pltpu.VMEM((2, 8, 128), F32),
            pltpu.VMEM((row_n - 1, 8, 128), F32),
            pltpu.VMEM((tm_n - 1, 8, 128), F32),
            pltpu.VMEM((8, 128), F32),
            dma((12,)),
            dma((8,)), dma((8,)),
            dma((row_n - 1,)), dma((row_n - 1,)),
            dma((tm_n - 1,)), dma((tm_n - 1,)),
            dma((10,)), dma((10,)),
            dma((4,)), dma((4,)),
            dma((14,)), dma((14,)),
        ],
        compiler_params=pltpu.CompilerParams(
            collective_id=0, has_side_effects=True, vmem_limit_bytes=56 * MIB
        ),
    )(features, aux, taps, embed_weight, mtok, pos, query_weight, key_weight, value_weight)
    smem = pl.BlockSpec(memory_space=pltpu.SMEM)
    out = pl.pallas_call(
        functools.partial(back, tm_n, row_n),
        name="back",
        out_shape=block,
        in_specs=[smem, smem] + [anywhere] * 9,
        out_specs=anywhere,
        scratch_shapes=[
            pltpu.SMEM((32,), jnp.int32),
            pltpu.SMEM((48,), jnp.int32),
            pltpu.VMEM((8, 128, 1024), BF16),
            pltpu.VMEM((24, 128, 1024), BF16),
            pltpu.VMEM((24, 128, 1024), BF16),
            pltpu.VMEM((6, 4, 32, 128), BF16),
            pltpu.VMEM((32, 2048), BF16),
            pltpu.VMEM((1, 2048), F32),
            pltpu.VMEM((2, 2048, 1024), BF16),
            pltpu.VMEM((16, 128, 2048), BF16),
            pltpu.VMEM((128, 2048), F32),
            pltpu.VMEM((256, 2048), BF16),
            pltpu.VMEM((8, 128, 1024), BF16),
            dma((14,)), dma((16,)), dma((8,)),
        ],
        compiler_params=pltpu.CompilerParams(vmem_limit_bytes=56 * MIB),
    )(pattern.reshape(8, 4), logit_scale, q, k, v, pos_halo, lat_halo, embed_weight, mtok, key_weight, value_weight)
    return out.reshape(4, 4, 64, 1024)


def solution(mesh):
    slab = ("tm", "row")
    return jax.shard_map(
        functools.partial(per_device, mesh.shape["tm"], mesh.shape["row"]),
        mesh=mesh,
        in_specs=(
            P(*slab, None, None), P(), P(), P(), P(), P(*slab, None), P(), P(), P(*slab, None, None),
            P(), P(), P(), P(), P(*slab, None),
        ),
        out_specs=P(*slab, None, None),
        check_vma=False,
    )
```

time: 313 us -> 175 us (0.56)
  the two profiles are of different devices: /device:TPU:11 before, /device:TPU:1 now
where the time goes in v1:
time: 175 us
  Pallas kernels  172 us (98%)
  other arithmetic  2.07 us (1%)
    pallas_call x1, Pallas kernels, per_device(): pl.pallas_call(functools.partial(front, tm_n, row_n), name='front', out_s...  120 us
    pallas_call x1, Pallas kernels, per_device(): pl.pallas_call(functools.partial(back, tm_n, row_n), name='back', out_sha...  52.2 us

profile of v1, /device:TPU:1, one launch (start us, length us, event | category | flops | bytes accessed | tf_op | source)
XLA Modules:
  0.0 175.2 jit_solution(10050485306394650864)
XLA Ops:
  0.0 0.7 pad.2.clone
  0.7 0.7 convert_element_type.6
  1.4 0.1 convert_element_type.7
  1.5 1.4 pad_maximum_fusion.aux
  2.9 120.2 %front.1 = (bf16[8,128,1024]{2,1,0:T(8,128)(2,1)}, bf16[8,128,1024]{2,1,0:T(8,128)(2,1)}, bf16[8,128,1024]{2,1,0:T(8,128)(2,1)}, bf16[6,4,128,2048]{3,2,1,0:T(8,128)(2,1)}, bf16[6,4,32,128]{3,2,1,0:T(8,128)(2,1)}) custom-call(bf16[4,4,64,512]{3,2,1,0:T(8,128)(2,1)} %feat.1, f32[32,128]{1,0:T(8,128)} %pad_maximum_fusion.aux, bf16[3,144,512]{2,1,0:T(8,128)(2,1)} %bitcast.10, ...), custom_call_target="tpu_custom_call" | custom-call | tf_op jit(solution)/shard_map/front/pallas_call | solution.py:443
  123.1 52.2 %back.1 = bf16[8,128,1024]{2,1,0:T(8,128)(2,1)} custom-call(s32[8,4]{1,0:T(8,128)} %bitcast.13, f32[8]{0:T(128)} %scale.1, bf16[8,128,1024]{2,1,0:T(8,128)(2,1)} %get-tuple-element.10.q, bf16[8,128,1024]{2,1,0:T(8,128)(2,1)} %get-tuple-element.11.k, bf16[8,128,1024]{2,1,0:T(8,128)(2,1)} %get-tuple-element.12.v, ...), custom_call_target="tpu_custom_call" | custom-call | tf_op jit(solution)/shard_map/back/pallas_call | solution.py:483

commit v2 on v1

v2 whole, which is shorter than its diff:
```python
import functools

import jax
import jax.numpy as jnp
from jax import lax
from jax.experimental import pallas as pl
from jax.experimental.pallas import tpu as pltpu
from jax.sharding import PartitionSpec as P

MESH = pl.DeviceIdType.MESH
F32, BF16 = jnp.float32, jnp.bfloat16
GROUP = 16
NT_DIMS = (((1,), (1,)), ((), ()))
TN_DIMS = (((0,), (0,)), ((), ()))
MIB = 1 << 20


def remote(src, dst, send, recv, tm, row):
    return pltpu.make_async_remote_copy(
        src_ref=src,
        dst_ref=dst,
        send_sem=send,
        recv_sem=recv,
        device_id={"tm": tm, "row": row},
        device_id_type=MESH,
    )


def group_sum(x):
    lane = lax.broadcasted_iota(jnp.int32, x.shape, 1)
    for k in (1, 2, 4, 8):
        down = pltpu.roll(x, 128 - k, 1)
        up = pltpu.roll(x, k, 1)
        x = x + jnp.where((lane & k) == 0, down, up)
    return x


def mask_rows(mask_token):
    hi = mask_token.astype(BF16).astype(F32)
    mid = (mask_token - hi).astype(BF16).astype(F32)
    low = mask_token - hi - mid
    row = lax.broadcasted_iota(jnp.int32, (16, mask_token.shape[1]), 0)
    zero = jnp.zeros(row.shape, F32)
    return jnp.where(row == 0, hi, jnp.where(row == 1, mid, jnp.where(row == 2, low, zero))).astype(BF16)


def layer_norm(tokens, pos):
    x = tokens + pos.astype(F32)
    c = x - jnp.mean(x, axis=-1, keepdims=True)
    return (c * lax.rsqrt(jnp.mean(c * c, axis=-1, keepdims=True) + 1e-05)).astype(BF16)


def head_norm(y):
    y = y.astype(BF16).astype(F32)
    parts = []
    for i in range(y.shape[1] // 128):
        part = y[:, 128 * i : 128 * (i + 1)]
        parts.append(part * lax.rsqrt(jnp.mean(part * part, axis=-1, keepdims=True) + 1e-06))
    return jnp.concatenate(parts, axis=1).astype(BF16)


def layer(
    tm_n, row_n,
    pattern, scale, feat, aux, taps, embed, mask_token, pos, wq, wk, wv,
    out,
    cells, act, aux_v, taps_v, emb_v, mtok_v, pos_v, w_v, hidden_a, hidden_b, tok, lat_v, q_v, k_v, v_v, out_v,
    mine, stat_r, stat_t, affine,
    load, o_sem, f_send, f_recv, r_send, r_recv, t_send, t_recv, p_send, p_recv, c_send, c_recv, l_send, l_recv,
):
    tm, row = lax.axis_index("tm"), lax.axis_index("row")

    def wrap(i, n):
        return lax.rem(i + n, n)

    before, after = wrap(tm - 1, tm_n), wrap(tm + 1, tm_n)
    above, below = wrap(row - 1, row_n), wrap(row + 1, row_n)

    own = pltpu.make_async_copy(feat, cells.at[1:5, 1:5], load.at[0])
    own.start()
    local = [
        pltpu.make_async_copy(aux, aux_v, load.at[1]),
        pltpu.make_async_copy(taps, taps_v, load.at[2]),
        pltpu.make_async_copy(embed, emb_v.at[0:16], load.at[3]),
        pltpu.make_async_copy(mask_token, mtok_v, load.at[4]),
        *[
            pltpu.make_async_copy(pos.at[2 * t : 2 * t + 2], pos_v.at[4 * t + 5 : 4 * t + 7], load.at[5 + t])
            for t in range(4)
        ],
        pltpu.make_async_copy(wq, w_v.at[0], load.at[9]),
        pltpu.make_async_copy(wk, w_v.at[1], load.at[10]),
        pltpu.make_async_copy(wv, w_v.at[2], load.at[11]),
    ]
    for copy in local:
        copy.start()

    barrier = pltpu.get_barrier_semaphore()
    for d in range(1, row_n):
        pl.semaphore_signal(barrier, inc=1, device_id={"tm": tm, "row": wrap(row + d, row_n)}, device_id_type=MESH)
    for d in range(1, tm_n):
        pl.semaphore_signal(barrier, inc=1, device_id={"tm": wrap(tm + d, tm_n), "row": row}, device_id_type=MESH)
    for t in (before, after):
        for r in (above, below):
            pl.semaphore_signal(barrier, inc=1, device_id={"tm": t, "row": r}, device_id_type=MESH)
    pl.semaphore_wait(barrier, row_n - 1 + tm_n - 1 + 4)

    halo = [
        (feat.at[:, 3], cells.at[1:5, 0], tm, below),
        (feat.at[:, 0], cells.at[1:5, 5], tm, above),
        (feat.at[3], cells.at[0, 1:5], after, row),
        (feat.at[0], cells.at[5, 1:5], before, row),
        (feat.at[3, 3], cells.at[0, 0], after, below),
        (feat.at[3, 0], cells.at[0, 5], after, above),
        (feat.at[0, 3], cells.at[5, 0], before, below),
        (feat.at[0, 0], cells.at[5, 5], before, above),
    ]
    feat_copies = [
        remote(src, dst, f_send.at[i], f_recv.at[i], t, r) for i, (src, dst, t, r) in enumerate(halo)
    ]
    for copy in feat_copies:
        copy.start()

    own.wait()
    half = jnp.zeros((8, 512), F32)

    def add_row(i, carry):
        total, square = carry
        x = cells[1 + i // 4, 1 + i % 4].astype(F32)
        for j in range(8):
            part = x[8 * j : 8 * (j + 1)]
            total, square = total + part, square + part * part
        return total, square

    total, square = lax.fori_loop(0, 16, add_row, (half, half))
    total = jnp.sum(total, axis=0, keepdims=True)
    square = jnp.sum(square, axis=0, keepdims=True)
    for i in range(4):
        mine[0, i : i + 1] = total[:, 128 * i : 128 * (i + 1)]
        mine[0, 4 + i : 5 + i] = square[:, 128 * i : 128 * (i + 1)]
    row_copies = [
        remote(mine.at[0], stat_r.at[d - 1], r_send.at[d - 1], r_recv.at[d - 1], tm, wrap(row + d, row_n))
        for d in range(1, row_n)
    ]
    for copy in row_copies:
        copy.start()
    for copy in row_copies:
        copy.wait_recv()
    mine[1] = mine[0] + jnp.sum(stat_r[...], axis=0)
    tm_copies = [
        remote(mine.at[1], stat_t.at[d - 1], t_send.at[d - 1], t_recv.at[d - 1], wrap(tm + d, tm_n), row)
        for d in range(1, tm_n)
    ]
    for copy in tm_copies:
        copy.start()
    for copy in tm_copies:
        copy.wait_recv()

    down, up = {}, {}
    for i, t in enumerate((0, 3, 1, 2)):
        down[t] = remote(pos.at[2 * t + 1], pos_v.at[4 * t + 4], p_send.at[i], p_recv.at[i], tm, below)
        up[t] = remote(pos.at[2 * t], pos_v.at[4 * t + 7], p_send.at[4 + i], p_recv.at[4 + i], tm, above)
    along = [
        remote(pos.at[6:8], pos_v.at[1:3], p_send.at[8], p_recv.at[8], after, row),
        remote(pos.at[0:2], pos_v.at[21:23], p_send.at[9], p_recv.at[9], before, row),
    ]
    first = [down[0], up[0], down[3], up[3], *along]
    second = [down[1], up[1], down[2], up[2]]
    for copy in first:
        copy.start()

    for copy in local[:5]:
        copy.wait()
    every = group_sum(mine[1] + jnp.sum(stat_t[...], axis=0))
    count = tm_n * row_n * 4 * 4 * 64 * GROUP
    average = every[0:4] / count
    variance = every[4:8] / count - average * average
    inverse = lax.rsqrt(variance + 1e-06)
    affine[0:4] = inverse * aux_v[0:4]
    affine[4:8] = aux_v[4:8] - average * inverse * aux_v[0:4]
    emb_v[16:32] = mask_rows(mtok_v[...])

    for copy in feat_copies:
        copy.wait_recv()

    def activate(i, _):
        f, r = i // 6, i % 6
        frame, line = tm * 4 + f - 1, row * 4 + r - 1
        inside = (frame >= 0) & (frame < tm_n * 4) & (line >= 0) & (line < row_n * 4)
        keep = jnp.where(inside, 0.5, 0.0)
        for j in range(4):
            lanes = slice(128 * j, 128 * (j + 1))
            v = cells[f, r, :, lanes].astype(F32) * affine[j : j + 1] + affine[4 + j : 5 + j]
            v = (v * keep) * (1.0 + jnp.tanh(0.5 * v))
            act[f, pl.ds(pl.multiple_of(r * 64, 64), 64), lanes] = v.astype(BF16)
        return 0

    lax.fori_loop(0, 36, activate, 0)

    column = lax.broadcasted_iota(jnp.int32, (16, 256), 1) % 64
    third = lax.broadcasted_iota(jnp.int32, (16, 128), 0) < 3

    def convolve(t, _):
        acc = jnp.zeros((144, 384), F32)
        for a in range(3):
            acc = acc + lax.dot_general(taps_v[a], act[t + a], NT_DIMS, preferred_element_type=F32)
        sums = []
        for c in range(3):
            part = acc[16 * c : 16 * c + 16]
            for b in (1, 2):
                part = part + pltpu.roll(acc[48 * b + 16 * c : 48 * b + 16 * c + 16], 384 - 64 * b, 1)
            sums.append(part[:, :256])
        left = jnp.where(column == 0, 0.0, pltpu.roll(sums[0], 1, 1))
        right = jnp.where(column == 63, 0.0, pltpu.roll(sums[2], 255, 1))
        out = sums[1] + left + right
        for p in range(2):
            masked = aux_v[pl.ds(24 + 2 * t + p, 1)]
            value = (out[:, 128 * p : 128 * (p + 1)] + aux_v[8:24]).astype(BF16).astype(F32)
            lat_v[4 * t + 5 + p, 0:16] = jnp.where(masked > 0.5, 0.0, value).astype(BF16)
            lat_v[4 * t + 5 + p, 16:32] = jnp.where(third, masked, 0.0).astype(BF16)
        return 0

    lax.fori_loop(0, 4, convolve, 0)

    lat_sends = []
    for t in range(4):
        lat_sends.append((lat_v.at[4 * t + 6], lat_v.at[4 * t + 4], tm, below))
        lat_sends.append((lat_v.at[4 * t + 5], lat_v.at[4 * t + 7], tm, above))
    lat_sends += [
        (lat_v.at[17:19], lat_v.at[1:3], after, row),
        (lat_v.at[5:7], lat_v.at[21:23], before, row),
        (lat_v.at[18], lat_v.at[0], after, below),
        (lat_v.at[17], lat_v.at[3], after, above),
        (lat_v.at[6], lat_v.at[20], before, below),
        (lat_v.at[5], lat_v.at[23], before, above),
    ]
    lat_copies = [remote(src, dst, l_send.at[i], l_recv.at[i], t, r) for i, (src, dst, t, r) in enumerate(lat_sends)]
    for copy in lat_copies:
        copy.start()
    for copy in second:
        copy.start()

    def spot_of(group, i):
        base, a, b = group
        return base + a * (i % 2) + b * (i // 2)

    def normalize(group, i, hidden):
        spot = spot_of(group, i)
        tok[...] = lax.dot_general(lat_v[spot], emb_v[...], TN_DIMS, preferred_element_type=F32)
        for c in range(4):
            rows = slice(32 * c, 32 * c + 32)
            hidden[pl.ds(pl.multiple_of(i * 128 + 32 * c, 32), 32)] = layer_norm(tok[rows], pos_v[spot, rows])

    def project(group, following, hidden, other, own):
        spots = [spot_of(group, j) for j in range(4)]

        def step(i, _):
            columns = pl.ds(pl.multiple_of(i * 256, 256), 256)
            if following is not None:
                normalize(following, i, other)
            if own is not None:
                y = head_norm(jnp.dot(hidden[...], w_v[0, :, columns], preferred_element_type=F32))
                q_v[4 * own : 4 * own + 4, :, columns] = y.reshape(4, 128, 256)
            y = head_norm(jnp.dot(hidden[...], w_v[1, :, columns], preferred_element_type=F32))
            for j in range(4):
                k_v[spots[j], :, columns] = y[128 * j : 128 * (j + 1)]
            y = jnp.dot(hidden[...], w_v[2, :, columns], preferred_element_type=F32).astype(BF16)
            for j in range(4):
                v_v[spots[j], :, columns] = y[128 * j : 128 * (j + 1)]
            return 0

        lax.fori_loop(0, 4, step, 0)

    own_0, own_1, sides = (5, 1, 4), (13, 1, 4), (1, 1, 20)
    ends, corners, middle = (4, 3, 12), (0, 3, 20), (8, 3, 4)
    for copy in local[5:]:
        copy.wait()

    def begin(i, _):
        normalize(own_0, i, hidden_a)
        return 0

    lax.fori_loop(0, 4, begin, 0)
    project(own_0, own_1, hidden_a, hidden_b, 0)
    for copy in [*along, *lat_copies]:
        copy.wait_recv()
    project(own_1, sides, hidden_b, hidden_a, 1)

    odd = lax.rem(row, 2)
    other = row + 1 - 2 * odd
    outer = 3 * odd
    for copy in first[:4]:
        copy.wait_recv()
    corner = [
        remote(pos_v.at[4 + outer], pos_v.at[20 + outer], c_send.at[0], c_recv.at[0], before, row),
        remote(pos_v.at[16 + outer], pos_v.at[outer], c_send.at[1], c_recv.at[1], after, row),
        remote(pos_v.at[2 - odd], pos_v.at[outer], c_send.at[2], c_recv.at[2], tm, other),
        remote(pos_v.at[22 - odd], pos_v.at[20 + outer], c_send.at[3], c_recv.at[3], tm, other),
    ]
    for copy in corner:
        copy.start()
    project(sides, ends, hidden_a, hidden_b, None)
    for copy in corner:
        copy.wait_recv()
    project(ends, corners, hidden_b, hidden_a, None)
    for copy in second:
        copy.wait_recv()
    project(corners, middle, hidden_a, hidden_b, None)
    project(middle, None, hidden_b, hidden_a, None)

    def attend(b, _):
        mine_at = 4 * (b // 2) + 5 + b % 2
        spots, live = [], []
        for s in range(4):
            listed = pattern[b, s]
            spot = (listed // (2 * row_n) - tm * 4 + 1) * 4 + listed % (2 * row_n) - row * 2 + 1
            spots.append(jnp.clip(jnp.where(listed >= 0, spot, mine_at), 0, 23))
            live.append(jnp.where(listed >= 0, 1.0, 0.0))

        def head(h, _):
            columns = pl.ds(pl.multiple_of(h * 128, 128), 128)
            keys = jnp.concatenate([k_v[spot, :, columns] for spot in spots], axis=0)
            values = jnp.concatenate([v_v[spot, :, columns] for spot in spots], axis=0)
            score = lax.dot_general(q_v[b, :, columns], keys, NT_DIMS, preferred_element_type=F32)
            factor = scale[h] / 128.0
            parts = [jnp.exp(score[:, 128 * s : 128 * (s + 1)] * factor) * live[s] for s in range(4)]
            total = jnp.sum((parts[0] + parts[1]) + (parts[2] + parts[3]), axis=-1, keepdims=True)
            weight = jnp.concatenate([part.astype(BF16) for part in parts], axis=1)
            acc = jnp.dot(weight, values, preferred_element_type=F32)
            out_v[b, :, columns] = (acc / total).astype(BF16)
            return 0

        lax.fori_loop(0, 8, head, 0, unroll=4)
        pltpu.make_async_copy(out_v.at[b], out.at[b], o_sem.at[b]).start()
        return 0

    lax.fori_loop(0, 8, attend, 0)
    for copy in [*feat_copies, *row_copies, *tm_copies, *first, *second, *lat_copies, *corner]:
        copy.wait_send()
    for b in range(8):
        pltpu.make_async_copy(out_v.at[b], out.at[b], o_sem.at[b]).wait()


def per_device(
    tm_n, row_n,
    features, norm_gain, norm_bias, latent_kernel, latent_bias, token_mask, embed_weight, mask_token, pos_embed,
    query_weight, key_weight, value_weight, logit_scale, pattern,
):
    taps = latent_kernel.transpose(1, 2, 3, 0, 4).reshape(3, 144, 512)
    aux = jnp.concatenate(
        [
            norm_gain.reshape(4, 128),
            norm_bias.reshape(4, 128),
            jnp.broadcast_to(latent_bias[:, None], (16, 128)),
            token_mask.reshape(8, 128).astype(F32),
        ]
    )
    pos = pos_embed.reshape(8, 128, 2048)
    mtok = mask_token.reshape(1, 2048)
    anywhere = pl.BlockSpec(memory_space=pl.ANY)
    dma = pltpu.SemaphoreType.DMA
    block = jax.ShapeDtypeStruct((8, 128, 1024), BF16)
    smem = pl.BlockSpec(memory_space=pltpu.SMEM)
    out = pl.pallas_call(
        functools.partial(layer, tm_n, row_n),
        name="layer",
        out_shape=block,
        in_specs=[smem, smem] + [anywhere] * 9,
        out_specs=anywhere,
        scratch_shapes=[
            pltpu.VMEM((6, 6, 64, 512), BF16),
            pltpu.VMEM((6, 384, 512), BF16),
            pltpu.VMEM((32, 128), F32),
            pltpu.VMEM((3, 144, 512), BF16),
            pltpu.VMEM((32, 2048), BF16),
            pltpu.VMEM((1, 2048), F32),
            pltpu.VMEM((24, 128, 2048), BF16),
            pltpu.VMEM((3, 2048, 1024), BF16),
            pltpu.VMEM((512, 2048), BF16),
            pltpu.VMEM((512, 2048), BF16),
            pltpu.VMEM((128, 2048), F32),
            pltpu.VMEM((24, 32, 128), BF16),
            pltpu.VMEM((8, 128, 1024), BF16),
            pltpu.VMEM((24, 128, 1024), BF16),
            pltpu.VMEM((24, 128, 1024), BF16),
            pltpu.VMEM((8, 128, 1024), BF16),
            pltpu.VMEM((2, 8, 128), F32),
            pltpu.VMEM((row_n - 1, 8, 128), F32),
            pltpu.VMEM((tm_n - 1, 8, 128), F32),
            pltpu.VMEM((8, 128), F32),
            dma((12,)), dma((8,)),
            dma((8,)), dma((8,)),
            dma((row_n - 1,)), dma((row_n - 1,)),
            dma((tm_n - 1,)), dma((tm_n - 1,)),
            dma((10,)), dma((10,)),
            dma((4,)), dma((4,)),
            dma((14,)), dma((14,)),
        ],
        compiler_params=pltpu.CompilerParams(collective_id=0, has_side_effects=True, vmem_limit_bytes=58 * MIB),
    )(
        pattern.reshape(8, 4), logit_scale, features, aux, taps, embed_weight, mtok, pos,
        query_weight, key_weight, value_weight,
    )
    return out.reshape(4, 4, 64, 1024)


def solution(mesh):
    slab = ("tm", "row")
    return jax.shard_map(
        functools.partial(per_device, mesh.shape["tm"], mesh.shape["row"]),
        mesh=mesh,
        in_specs=(
            P(*slab, None, None), P(), P(), P(), P(), P(*slab, None), P(), P(), P(*slab, None, None),
            P(), P(), P(), P(), P(*slab, None),
        ),
        out_specs=P(*slab, None, None),
        check_vma=False,
    )
```

time: 175 us -> 156 us (0.89)
  the two profiles are of different devices: /device:TPU:1 before, /device:TPU:11 now
where the time goes in v2:
time: 156 us; the launch traced here: 153 us
  Pallas kernels  147 us (94%)
  local copies, waits for them, and re-layouts  3.95 us (3%)
  other arithmetic  2.07 us (1%)
    pallas_call x1, Pallas kernels, per_device(): pl.pallas_call(functools.partial(layer, tm_n, row_n), name='layer', out_s...  147 us
    unnamed x1, local copies, waits for them, and re-layouts  3.14 us

profile of v2, /device:TPU:11, one launch (start us, length us, event | category | flops | bytes accessed | tf_op | source)
XLA Modules:
  0.0 153.1 jit_solution(10301487267586952947)
XLA Ops:
  0.0 0.7 pad.2.clone
  0.7 0.7 convert_element_type.6
  1.4 0.1 convert_element_type.7
  1.5 1.4 pad_maximum_fusion.aux
  2.9 147.1 %layer.1 = bf16[8,128,1024]{2,1,0:T(8,128)(2,1)} custom-call(s32[8,4]{1,0:T(8,128)} %bitcast.13, f32[8]{0:T(128)} %scale.1, bf16[4,4,64,512]{3,2,1,0:T(8,128)(2,1)} %feat.1, f32[32,128]{1,0:T(8,128)} %pad_maximum_fusion.aux, bf16[3,144,512]{2,1,0:T(8,128)(2,1)} %bitcast.11, bf16[16,2048]{1,0:T(8,128)(2,1)} %embed.1, f32[1,2048]{1,0:T(1,128)} %bitcast.12, ...), custom_call_target="tpu_custom_call" | custom-call | tf_op jit(solution)/shard_map/layer/pallas_call | solution.py:362
  149.9 3.1 %copy.16 = bf16[4,4,64,1024]{3,2,1,0:T(8,128)(2,1)} copy(bf16[4,4,64,1024]{3,2,1,0:T(8,128)(2,1)} %bitcast.9) | data formatting | bytes 4194304

commit v3 on v2

--- a/solution.py
+++ b/solution.py
@@ -103,6 +103,71 @@
             pl.semaphore_signal(barrier, inc=1, device_id={"tm": t, "row": r}, device_id_type=MESH)
     pl.semaphore_wait(barrier, row_n - 1 + tm_n - 1 + 4)
 
+    last, low, high = tm_n - 1, tm_n // 2 - 1, tm_n // 2
+    down, up = {}, {}
+    for i, t in enumerate((0, 3, 1, 2)):
+        down[t] = remote(pos.at[2 * t + 1], pos_v.at[4 * t + 4], p_send.at[i], p_recv.at[i], tm, below)
+        up[t] = remote(pos.at[2 * t], pos_v.at[4 * t + 7], p_send.at[4 + i], p_recv.at[4 + i], tm, above)
+    at_low, at_high = (tm == low).astype(jnp.int32), (tm == high).astype(jnp.int32)
+    to_after = [
+        remote(pos.at[6], pos_v.at[1], p_send.at[8], p_recv.at[8], jnp.where(tm == low, 0, after), row),
+        remote(
+            pos.at[7], pos_v.at[2 + 20 * at_low], p_send.at[9], p_recv.at[9 + 2 * at_low],
+            jnp.where(tm == low, last, after), row,
+        ),
+    ]
+    to_before = [
+        remote(
+            pos.at[0], pos_v.at[21 - 19 * at_high], p_send.at[10], p_recv.at[10 - at_high],
+            jnp.where(tm == high, 0, before), row,
+        ),
+        remote(
+            pos.at[1], pos_v.at[22 - at_high], p_send.at[11], p_recv.at[11 - at_high],
+            jnp.where(tm == high, last, before), row,
+        ),
+    ]
+    from_first = [
+        remote(pos_v.at[1], pos_v.at[1], p_send.at[10], p_recv.at[8], high, row),
+        remote(pos_v.at[2], pos_v.at[21], p_send.at[11], p_recv.at[10], low, row),
+    ]
+    from_last = [
+        remote(pos_v.at[22], pos_v.at[2], p_send.at[8], p_recv.at[9], high, row),
+        remote(pos_v.at[21], pos_v.at[22], p_send.at[9], p_recv.at[11], low, row),
+    ]
+    arrive_before = [remote(pos.at[i], pos_v.at[1 + i], p_send.at[8 + i], p_recv.at[8 + i], last - tm, row) for i in range(2)]
+    arrive_after = [remote(pos.at[i], pos_v.at[21 + i], p_send.at[10 + i], p_recv.at[10 + i], last - tm, row) for i in range(2)]
+
+    def start_along():
+        @pl.when(tm != last)
+        def _():
+            for copy in to_after:
+                copy.start()
+
+        @pl.when(tm != 0)
+        def _():
+            for copy in to_before:
+                copy.start()
+
+    def start_frames(*frames):
+        for t in frames:
+            down[t].start()
+            up[t].start()
+
+    def relay_positions():
+        @pl.when(tm == 0)
+        def _():
+            for copy in arrive_before:
+                copy.wait_recv()
+            for copy in from_first:
+                copy.start()
+
+        @pl.when(tm == last)
+        def _():
+            for copy in arrive_after:
+                copy.wait_recv()
+            for copy in from_last:
+                copy.start()
+
     halo = [
         (feat.at[:, 3], cells.at[1:5, 0], tm, below),
         (feat.at[:, 0], cells.at[1:5, 5], tm, above),
@@ -151,21 +216,9 @@
     ]
     for copy in tm_copies:
         copy.start()
+    start_frames(0)
     for copy in tm_copies:
         copy.wait_recv()
-
-    down, up = {}, {}
-    for i, t in enumerate((0, 3, 1, 2)):
-        down[t] = remote(pos.at[2 * t + 1], pos_v.at[4 * t + 4], p_send.at[i], p_recv.at[i], tm, below)
-        up[t] = remote(pos.at[2 * t], pos_v.at[4 * t + 7], p_send.at[4 + i], p_recv.at[4 + i], tm, above)
-    along = [
-        remote(pos.at[6:8], pos_v.at[1:3], p_send.at[8], p_recv.at[8], after, row),
-        remote(pos.at[0:2], pos_v.at[21:23], p_send.at[9], p_recv.at[9], before, row),
-    ]
-    first = [down[0], up[0], down[3], up[3], *along]
-    second = [down[1], up[1], down[2], up[2]]
-    for copy in first:
-        copy.start()
 
     for copy in local[:5]:
         copy.wait()
@@ -235,8 +288,8 @@
     lat_copies = [remote(src, dst, l_send.at[i], l_recv.at[i], t, r) for i, (src, dst, t, r) in enumerate(lat_sends)]
     for copy in lat_copies:
         copy.start()
-    for copy in second:
-        copy.start()
+    start_along()
+    start_frames(3, 1, 2)
 
     def spot_of(group, i):
         base, a, b = group
@@ -274,37 +327,59 @@
     for copy in local[5:]:
         copy.wait()
 
-    def begin(i, _):
-        normalize(own_0, i, hidden_a)
-        return 0
-
-    lax.fori_loop(0, 4, begin, 0)
+    def begin(group):
+        def one(i, _):
+            normalize(group, i, hidden_a)
+            return 0
+
+        lax.fori_loop(0, 4, one, 0)
+
+    begin(own_0)
     project(own_0, own_1, hidden_a, hidden_b, 0)
-    for copy in [*along, *lat_copies]:
+    project(own_1, None, hidden_b, hidden_a, 1)
+    relay_positions()
+    for copy in lat_copies:
         copy.wait_recv()
-    project(own_1, sides, hidden_b, hidden_a, 1)
+
+    @pl.when(tm != 0)
+    def _():
+        for copy in arrive_before:
+            copy.wait_recv()
+
+    @pl.when(tm != last)
+    def _():
+        for copy in arrive_after:
+            copy.wait_recv()
+
+    begin(sides)
 
     odd = lax.rem(row, 2)
     other = row + 1 - 2 * odd
     outer = 3 * odd
-    for copy in first[:4]:
-        copy.wait_recv()
-    corner = [
-        remote(pos_v.at[4 + outer], pos_v.at[20 + outer], c_send.at[0], c_recv.at[0], before, row),
-        remote(pos_v.at[16 + outer], pos_v.at[outer], c_send.at[1], c_recv.at[1], after, row),
+    for t in (0, 3):
+        down[t].wait_recv()
+        up[t].wait_recv()
+    outer_before = remote(pos_v.at[4 + outer], pos_v.at[20 + outer], c_send.at[0], c_recv.at[0], before, row)
+    outer_after = remote(pos_v.at[16 + outer], pos_v.at[outer], c_send.at[1], c_recv.at[1], after, row)
+    inner = [
         remote(pos_v.at[2 - odd], pos_v.at[outer], c_send.at[2], c_recv.at[2], tm, other),
         remote(pos_v.at[22 - odd], pos_v.at[20 + outer], c_send.at[3], c_recv.at[3], tm, other),
     ]
-    for copy in corner:
+    pl.when(tm != 0)(outer_before.start)
+    pl.when(tm != last)(outer_after.start)
+    for copy in inner:
         copy.start()
     project(sides, ends, hidden_a, hidden_b, None)
-    for copy in corner:
+    for t in (1, 2):
+        down[t].wait_recv()
+        up[t].wait_recv()
+    project(ends, middle, hidden_b, hidden_a, None)
+    for copy in inner:
         copy.wait_recv()
-    project(ends, corners, hidden_b, hidden_a, None)
-    for copy in second:
-        copy.wait_recv()
-    project(corners, middle, hidden_a, hidden_b, None)
-    project(middle, None, hidden_b, hidden_a, None)
+    pl.when(tm != last)(outer_before.wait_recv)
+    pl.when(tm != 0)(outer_after.wait_recv)
+    project(middle, corners, hidden_a, hidden_b, None)
+    project(corners, None, hidden_b, hidden_a, None)
 
     def attend(b, _):
         mine_at = 4 * (b // 2) + 5 + b % 2
@@ -315,26 +390,33 @@
             spots.append(jnp.clip(jnp.where(listed >= 0, spot, mine_at), 0, 23))
             live.append(jnp.where(listed >= 0, 1.0, 0.0))
 
-        def head(h, _):
-            columns = pl.ds(pl.multiple_of(h * 128, 128), 128)
-            keys = jnp.concatenate([k_v[spot, :, columns] for spot in spots], axis=0)
-            values = jnp.concatenate([v_v[spot, :, columns] for spot in spots], axis=0)
-            score = lax.dot_general(q_v[b, :, columns], keys, NT_DIMS, preferred_element_type=F32)
-            factor = scale[h] / 128.0
-            parts = [jnp.exp(score[:, 128 * s : 128 * (s + 1)] * factor) * live[s] for s in range(4)]
-            total = jnp.sum((parts[0] + parts[1]) + (parts[2] + parts[3]), axis=-1, keepdims=True)
-            weight = jnp.concatenate([part.astype(BF16) for part in parts], axis=1)
-            acc = jnp.dot(weight, values, preferred_element_type=F32)
-            out_v[b, :, columns] = (acc / total).astype(BF16)
+        def heads(g, _):
+            columns = [pl.ds(pl.multiple_of(g * 1024 + 128 * u, 128), 128) for u in range(8)]
+            scores = []
+            for u in range(8):
+                keys = jnp.concatenate([k_v[spot, :, columns[u]] for spot in spots], axis=0)
+                scores.append(lax.dot_general(q_v[b, :, columns[u]], keys, NT_DIMS, preferred_element_type=F32))
+            weights, totals = [], []
+            for u in range(8):
+                factor = scale[g * 8 + u] / 128.0
+                parts = [jnp.exp(scores[u][:, 128 * s : 128 * (s + 1)] * factor) * live[s] for s in range(4)]
+                totals.append(jnp.sum((parts[0] + parts[1]) + (parts[2] + parts[3]), axis=-1, keepdims=True))
+                weights.append(jnp.concatenate([part.astype(BF16) for part in parts], axis=1))
+            for u in range(8):
+                values = jnp.concatenate([v_v[spot, :, columns[u]] for spot in spots], axis=0)
+                acc = jnp.dot(weights[u], values, preferred_element_type=F32)
+                out_v[b, :, columns[u]] = (acc / totals[u]).astype(BF16)
             return 0
 
-        lax.fori_loop(0, 8, head, 0, unroll=4)
+        lax.fori_loop(0, 1, heads, 0)
         pltpu.make_async_copy(out_v.at[b], out.at[b], o_sem.at[b]).start()
         return 0
 
     lax.fori_loop(0, 8, attend, 0)
-    for copy in [*feat_copies, *row_copies, *tm_copies, *first, *second, *lat_copies, *corner]:
+    for copy in [*feat_copies, *row_copies, *tm_copies, *down.values(), *up.values(), *to_after, *to_before, *lat_copies, *inner]:
         copy.wait_send()
+    pl.when(tm != 0)(outer_before.wait_send)
+    pl.when(tm != last)(outer_after.wait_send)
     for b in range(8):
         pltpu.make_async_copy(out_v.at[b], out.at[b], o_sem.at[b]).wait()
 
@@ -390,7 +472,7 @@
             dma((8,)), dma((8,)),
             dma((row_n - 1,)), dma((row_n - 1,)),
             dma((tm_n - 1,)), dma((tm_n - 1,)),
-            dma((10,)), dma((10,)),
+            dma((12,)), dma((12,)),
             dma((4,)), dma((4,)),
             dma((14,)), dma((14,)),
         ],

time: 156 us -> 130 us (0.83); the launches traced: 153 us -> 129 us
  Pallas kernels: 147 us -> 123 us
    pallas_call x1, Pallas kernels: 147 us -> 123 us  [per_device(): pl.pallas_call(functools.partial(layer, tm_n, row_n), name='layer', out_s...]
where the time goes in v3:
time: 130 us; the launch traced here: 129 us
  Pallas kernels  123 us (95%)
  local copies, waits for them, and re-layouts  3.95 us (3%)
  other arithmetic  2.07 us (2%)
    pallas_call x1, Pallas kernels, per_device(): pl.pallas_call(functools.partial(layer, tm_n, row_n), name='layer', out_s...  123 us
    unnamed x1, local copies, waits for them, and re-layouts  3.14 us

profile of v3, /device:TPU:11, one launch (start us, length us, event | category | flops | bytes accessed | tf_op | source)
XLA Modules:
  0.0 129.4 jit_solution(15645251457907572914)
XLA Ops:
  0.0 0.7 pad.2.clone
  0.7 0.7 convert_element_type.6
  1.4 0.1 convert_element_type.7
  1.5 1.4 %pad_maximum_fusion.aux = f32[32,128]{1,0:T(8,128)} fusion(f32[8,128]{1,0:T(8,128)S(1)} %convert_element_type.7, f32[4,128]{1,0:T(4,128)} %bitcast.14, f32[4,128]{1,0:T(4,128)} %bitcast.15, f32[32]{0:T(128)S(1)} %pad.2.clone), kind=kLoop, calls=%fused_computation | loop fusion | flops 12288 | bytes 24704 | tf_op jit(solution)/shard_map/concatenate | solution.py:430
  2.9 123.4 %layer.1 = bf16[8,128,1024]{2,1,0:T(8,128)(2,1)} custom-call(s32[8,4]{1,0:T(8,128)} %bitcast.13, f32[8]{0:T(128)} %scale.1, bf16[4,4,64,512]{3,2,1,0:T(8,128)(2,1)} %feat.1, f32[32,128]{1,0:T(8,128)} %pad_maximum_fusion.aux, bf16[3,144,512]{2,1,0:T(8,128)(2,1)} %bitcast.11, bf16[16,2048]{1,0:T(8,128)(2,1)} %embed.1, f32[1,2048]{1,0:T(1,128)} %bitcast.12, ...), custom_call_target="tpu_custom_call" | custom-call | tf_op jit(solution)/shard_map/layer/pallas_call | solution.py:444
  126.3 3.1 %copy.16 = bf16[4,4,64,1024]{3,2,1,0:T(8,128)(2,1)} copy(bf16[4,4,64,1024]{3,2,1,0:T(8,128)(2,1)} %bitcast.9) | data formatting | bytes 4194304

commit v4 on v3

--- a/solution.py
+++ b/solution.py
@@ -289,7 +289,7 @@
     for copy in lat_copies:
         copy.start()
     start_along()
-    start_frames(3, 1, 2)
+    start_frames(3)
 
     def spot_of(group, i):
         base, a, b = group
@@ -336,29 +336,18 @@
 
     begin(own_0)
     project(own_0, own_1, hidden_a, hidden_b, 0)
+    start_frames(1, 2)
     project(own_1, None, hidden_b, hidden_a, 1)
     relay_positions()
     for copy in lat_copies:
         copy.wait_recv()
-
-    @pl.when(tm != 0)
-    def _():
-        for copy in arrive_before:
-            copy.wait_recv()
-
-    @pl.when(tm != last)
-    def _():
-        for copy in arrive_after:
-            copy.wait_recv()
-
-    begin(sides)
+    for t in (0, 3):
+        down[t].wait_recv()
+        up[t].wait_recv()
 
     odd = lax.rem(row, 2)
     other = row + 1 - 2 * odd
     outer = 3 * odd
-    for t in (0, 3):
-        down[t].wait_recv()
-        up[t].wait_recv()
     outer_before = remote(pos_v.at[4 + outer], pos_v.at[20 + outer], c_send.at[0], c_recv.at[0], before, row)
     outer_after = remote(pos_v.at[16 + outer], pos_v.at[outer], c_send.at[1], c_recv.at[1], after, row)
     inner = [
@@ -367,19 +356,32 @@
     ]
     pl.when(tm != 0)(outer_before.start)
     pl.when(tm != last)(outer_after.start)
+    begin(ends)
+    project(ends, None, hidden_a, hidden_b, None)
+
+    @pl.when(tm != 0)
+    def _():
+        for copy in arrive_before:
+            copy.wait_recv()
+
+    @pl.when(tm != last)
+    def _():
+        for copy in arrive_after:
+            copy.wait_recv()
+
     for copy in inner:
         copy.start()
-    project(sides, ends, hidden_a, hidden_b, None)
+    begin(sides)
     for t in (1, 2):
         down[t].wait_recv()
         up[t].wait_recv()
-    project(ends, middle, hidden_b, hidden_a, None)
+    project(sides, middle, hidden_a, hidden_b, None)
     for copy in inner:
         copy.wait_recv()
     pl.when(tm != last)(outer_before.wait_recv)
     pl.when(tm != 0)(outer_after.wait_recv)
-    project(middle, corners, hidden_a, hidden_b, None)
-    project(corners, None, hidden_b, hidden_a, None)
+    project(middle, corners, hidden_b, hidden_a, None)
+    project(corners, None, hidden_a, hidden_b, None)
 
     def attend(b, _):
         mine_at = 4 * (b // 2) + 5 + b % 2

time: 130 us -> 127 us (0.977)
  Pallas kernels: 123 us -> 120 us
    pallas_call x1, Pallas kernels: 123 us -> 120 us  [per_device(): pl.pallas_call(functools.partial(layer, tm_n, row_n), name='layer', out_s...]
where the time goes in v4:
time: 127 us; the launch traced here: 126 us
  Pallas kernels  120 us (94%)
  local copies, waits for them, and re-layouts  3.95 us (3%)
  other arithmetic  2.07 us (2%)
    pallas_call x1, Pallas kernels, per_device(): pl.pallas_call(functools.partial(layer, tm_n, row_n), name='layer', out_s...  120 us
    unnamed x1, local copies, waits for them, and re-layouts  3.14 us

profile of v4, /device:TPU:11, one launch (start us, length us, event | category | flops | bytes accessed | tf_op | source)
XLA Modules:
  0.0 125.6 jit_solution(13286279543453236604)
XLA Ops:
  0.0 0.7 pad.2.clone
  0.7 0.7 convert_element_type.6
  1.4 0.1 convert_element_type.7
  1.5 1.4 %pad_maximum_fusion.aux = f32[32,128]{1,0:T(8,128)} fusion(f32[8,128]{1,0:T(8,128)S(1)} %convert_element_type.7, f32[4,128]{1,0:T(4,128)} %bitcast.14, f32[4,128]{1,0:T(4,128)} %bitcast.15, f32[32]{0:T(128)S(1)} %pad.2.clone), kind=kLoop, calls=%fused_computation | loop fusion | flops 12288 | bytes 24704 | tf_op jit(solution)/shard_map/concatenate | solution.py:432
  2.9 119.6 %layer.1 = bf16[8,128,1024]{2,1,0:T(8,128)(2,1)} custom-call(s32[8,4]{1,0:T(8,128)} %bitcast.13, f32[8]{0:T(128)} %scale.1, bf16[4,4,64,512]{3,2,1,0:T(8,128)(2,1)} %feat.1, f32[32,128]{1,0:T(8,128)} %pad_maximum_fusion.aux, bf16[3,144,512]{2,1,0:T(8,128)(2,1)} %bitcast.11, bf16[16,2048]{1,0:T(8,128)(2,1)} %embed.1, f32[1,2048]{1,0:T(1,128)} %bitcast.12, ...), custom_call_target="tpu_custom_call" | custom-call | tf_op jit(solution)/shard_map/layer/pallas_call | solution.py:446
  122.4 3.1 %copy.16 = bf16[4,4,64,1024]{3,2,1,0:T(8,128)(2,1)} copy(bf16[4,4,64,1024]{3,2,1,0:T(8,128)(2,1)} %bitcast.9) | data formatting | bytes 4194304

commit v5 on v4

--- a/solution.py
+++ b/solution.py
@@ -195,7 +195,7 @@
             total, square = total + part, square + part * part
         return total, square
 
-    total, square = lax.fori_loop(0, 16, add_row, (half, half))
+    total, square = lax.fori_loop(0, 16, add_row, (half, half), unroll=2)
     total = jnp.sum(total, axis=0, keepdims=True)
     square = jnp.sum(square, axis=0, keepdims=True)
     for i in range(4):
@@ -246,7 +246,7 @@
             act[f, pl.ds(pl.multiple_of(r * 64, 64), 64), lanes] = v.astype(BF16)
         return 0
 
-    lax.fori_loop(0, 36, activate, 0)
+    lax.fori_loop(0, 36, activate, 0, unroll=2)
 
     column = lax.broadcasted_iota(jnp.int32, (16, 256), 1) % 64
     third = lax.broadcasted_iota(jnp.int32, (16, 128), 0) < 3
@@ -271,7 +271,7 @@
             lat_v[4 * t + 5 + p, 16:32] = jnp.where(third, masked, 0.0).astype(BF16)
         return 0
 
-    lax.fori_loop(0, 4, convolve, 0)
+    lax.fori_loop(0, 4, convolve, 0, unroll=2)
 
     lat_sends = []
     for t in range(4):

time: 127 us -> 127 us (level)
  no operation moved by 1% of the time
where the time goes in v5:
time: 127 us; the launch traced here: 126 us
  Pallas kernels  120 us (94%)
  local copies, waits for them, and re-layouts  3.95 us (3%)
  other arithmetic  2.07 us (2%)
    pallas_call x1, Pallas kernels, per_device(): pl.pallas_call(functools.partial(layer, tm_n, row_n), name='layer', out_s...  120 us
    unnamed x1, local copies, waits for them, and re-layouts  3.14 us

profile of v5, /device:TPU:11, one launch (start us, length us, event | category | flops | bytes accessed | tf_op | source)
XLA Modules:
  0.0 125.6 jit_solution(68621307805820357)
XLA Ops:
  0.0 0.7 pad.2.clone
  0.7 0.7 convert_element_type.6
  1.4 0.1 convert_element_type.7
  1.5 1.4 %pad_maximum_fusion.aux = f32[32,128]{1,0:T(8,128)} fusion(f32[8,128]{1,0:T(8,128)S(1)} %convert_element_type.7, f32[4,128]{1,0:T(4,128)} %bitcast.14, f32[4,128]{1,0:T(4,128)} %bitcast.15, f32[32]{0:T(128)S(1)} %pad.2.clone), kind=kLoop, calls=%fused_computation | loop fusion | flops 12288 | bytes 24704 | tf_op jit(solution)/shard_map/concatenate | solution.py:432
  2.9 119.5 %layer.1 = bf16[8,128,1024]{2,1,0:T(8,128)(2,1)} custom-call(s32[8,4]{1,0:T(8,128)} %bitcast.13, f32[8]{0:T(128)} %scale.1, bf16[4,4,64,512]{3,2,1,0:T(8,128)(2,1)} %feat.1, f32[32,128]{1,0:T(8,128)} %pad_maximum_fusion.aux, bf16[3,144,512]{2,1,0:T(8,128)(2,1)} %bitcast.11, bf16[16,2048]{1,0:T(8,128)(2,1)} %embed.1, f32[1,2048]{1,0:T(1,128)} %bitcast.12, ...), custom_call_target="tpu_custom_call" | custom-call | tf_op jit(solution)/shard_map/layer/pallas_call | solution.py:446
  122.4 3.1 %copy.16 = bf16[4,4,64,1024]{3,2,1,0:T(8,128)(2,1)} copy(bf16[4,4,64,1024]{3,2,1,0:T(8,128)(2,1)} %bitcast.9) | data formatting | bytes 4194304
